TPU v7x, 32 devices: a whole 2x2x4 slice. The times are simulated.
32 devices in a mesh: groups: 2 (over x), samp: 8 (over z, y), line: 2 (over core).
Axes of the slice: x: 2, y: 2, z: 4, core: 2. Of those that a mesh axis runs over, the one named last changes fastest.
Arguments:
- cube: float32 [7077888], P(('groups', 'samp', 'line')), parts along dimension 0, may hold values from -4000 to 4000
Outputs:
- details1: float32 [5308416], P(('groups', 'samp', 'line')), parts along dimension 0
- details2: float32 [1327104], P(('groups', 'samp', 'line')), parts along dimension 0
- details3: float32 [331776], P(('groups', 'samp', 'line')), parts along dimension 0
- approx: float32 [110592], P(('groups', 'samp', 'line')), parts along dimension 0
There are 2 independent parts, one for each index of `groups`. A program takes and returns all parts, laid end to end along the dimension named above; each array names one. Nothing has to cross between parts.
All inputs are finite; a program needn't handle non-finite values.
Results may differ from a plain program's by a relative error of at most 0.000088.
Values sent between devices are 32-bit elements; how exact they have to be, the bound alone decides.
No kernel may reach another device: no remote copies, remote signals or barrier semaphores. Data moves between devices by JAX's collectives and lax.ppermute only.
A program may use at most 64 MiB of HBM per device.

v0:
```python
import functools

import numpy as np
import jax
import jax.numpy as jnp
from jax import lax
from jax.experimental import pallas as pl
from jax.experimental.pallas import tpu as pltpu
from jax.sharding import PartitionSpec as P

BANDS = 432
LD = 32
SD = 16
LANES = 128
BLOCK = 128

alpha_lift = -1.586134342059924
beta_lift = -0.052980118572961
gamma_lift = 0.882911075530934
delta_lift = 0.443506852043971
scale_lift = 1.230174104914001

HIGHEST = lax.Precision.HIGHEST


def product(left, right, left_dim, right_dim):
    return lax.dot_general(
        left,
        right,
        (((left_dim,), (right_dim,)), ((), ())),
        precision=HIGHEST,
        preferred_element_type=jnp.float32,
    )


def lift_rows(values):
    evens, odds = values[0::2], values[1::2]
    for weight_odd, weight_even in ((alpha_lift, beta_lift), (gamma_lift, delta_lift)):
        following = np.concatenate([evens[1:], evens[-1:]])
        odds = odds + weight_odd * (evens + following)
        preceding = np.concatenate([odds[:1], odds[:-1]])
        evens = evens + weight_even * (preceding + odds)
    return evens / scale_lift, odds * scale_lift


def axis_operators(length):
    operators = {}
    current = np.eye(length)
    for level in (1, 2, 3):
        low, high = lift_rows(current)
        operators[level, 0], operators[level, 1] = low, high
        current = low
    return operators


def output_lanes():
    lanes = []
    for level in (1, 2, 3):
        parts = [(1, 0), (0, 1), (1, 1)] + ([(0, 0)] if level == 3 else [])
        for line_part, samp_part in parts:
            for line in range(LD >> level):
                for samp in range(SD >> level):
                    lanes.append((level, line_part, samp_part, line, samp))
    return lanes


def factor_tables(n_samp, n_line):
    lanes = output_lanes()
    line_ops = axis_operators(LD * n_line)
    samp_ops = axis_operators(SD * n_samp)
    count = len(lanes)
    line_table = np.zeros((n_line, n_line * LD, count))
    for q in range(n_line):
        order = [q] + [other for other in range(n_line) if other != q]
        for o, (level, part, _, line, _) in enumerate(lanes):
            row = line_ops[level, part][q * (LD >> level) + line]
            for k, source in enumerate(order):
                line_table[q, k * LD : (k + 1) * LD, o] = row[source * LD : (source + 1) * LD]
    reach = {}
    for step in (0, -1, 1, -2, 2):
        table = np.zeros((n_samp, SD, count))
        for p in range(n_samp):
            target = p + step
            if 0 <= target < n_samp:
                for o, (level, _, part, _, samp) in enumerate(lanes):
                    row = samp_ops[level, part][target * (SD >> level) + samp]
                    table[p, :, o] = row[p * SD : (p + 1) * SD]
        reach[step] = table
    return line_table, reach


SENDS = ((-1, 256), (1, 256), (-2, 128), (2, 128))


def build_constants(n_samp, n_line):
    line_table, reach = factor_tables(n_samp, n_line)
    count = line_table.shape[2]
    line_parts, samp_parts = [line_table], [reach[0]]
    selections, offsets = [], []
    line_sums = line_table.sum(1)
    for step, width in SENDS:
        used = np.nonzero(np.abs(reach[step]).sum((0, 1)))[0]
        assert len(used) < width
        line_cols = np.zeros((n_line, n_line * LD, width))
        samp_cols = np.zeros((n_samp, SD, width))
        line_cols[:, :, : len(used)] = line_table[:, :, used]
        samp_cols[:, :, : len(used)] = reach[step][:, :, used]
        line_parts.append(line_cols)
        samp_parts.append(samp_cols)
        chosen = np.full((width, 1), -1, np.int32)
        chosen[: len(used), 0] = used
        selections.append(np.broadcast_to(chosen, (width, LANES)))
        sums = np.zeros((n_samp, count))
        for p in range(n_samp):
            if 0 <= p - step < n_samp:
                sums[p] = reach[step][p - step].sum(0)
        offsets.append(sums)
    whole = np.zeros((n_samp, count))
    for p in range(n_samp):
        for step in reach:
            if 0 <= p - step < n_samp:
                whole[p] += reach[step][p - step].sum(0)
    offsets.append(whole)
    offset_table = np.zeros((n_samp, n_line, 8, count))
    for k, sums in enumerate(offsets):
        offset_table[:, :, k] = sums[:, None] * line_sums[None]
    return (
        np.concatenate(line_parts, 2).astype(np.float32),
        np.concatenate(samp_parts, 2).astype(np.float32),
        np.concatenate(selections, 0).astype(np.int32),
        offset_table.astype(np.float32),
    )


EDGES = list(range(0, BANDS, BLOCK)) + [BANDS]
LAST = EDGES[-1] - EDGES[-2]
OFF_DIAGONAL = ((1, 0), (2, 0), (2, 1), (3, 0), (3, 1), (3, 2))


def payload_rows(tiles):
    places = {}
    row = 2 * BLOCK
    for i, j in OFF_DIAGONAL:
        places[i, j] = row
        row += EDGES[i + 1] - EDGES[i]
    places["diagonal"] = row
    row += 8
    places["means"] = row
    row += 4 * tiles
    return places, -(-row // 32) * 32


def square_iotas():
    rows = lax.broadcasted_iota(jnp.int32, (BLOCK, BLOCK), 0)
    cols = lax.broadcasted_iota(jnp.int32, (BLOCK, BLOCK), 1)
    return rows, cols


def gram_kernel(tiles, where_ref, x_ref, send_ref, keep_ref, mean_ref, xs, pack):
    places, total = payload_rows(tiles)
    half = total // 2
    tile, line = where_ref[0], where_ref[1]
    per_row = LD * SD // LANES
    parts = [x_ref[pl.ds(c, BANDS, stride=per_row), :] for c in range(per_row)]
    mean = jnp.sum(sum(parts[1:], parts[0]), axis=1, keepdims=True) / (LD * SD)
    mean_ref[...] = jnp.broadcast_to(mean, (BANDS, LANES))
    for c in range(per_row):
        xs[0:BANDS, c * LANES : (c + 1) * LANES] = parts[c] - mean
    xs[BANDS:, :] = jnp.zeros_like(xs[BANDS:, :])
    rows, cols = square_iotas()

    def block(i, j):
        return product(
            xs[i * BLOCK : (i + 1) * BLOCK, :], xs[j * BLOCK : (j + 1) * BLOCK, :], 1, 1
        )

    pack[places["diagonal"] :, :] = jnp.zeros_like(pack[places["diagonal"] :, :])
    for k in range(2):
        lower, upper = block(2 * k, 2 * k), block(2 * k + 1, 2 * k + 1)
        pack[k * BLOCK : (k + 1) * BLOCK, :] = jnp.where(rows >= cols, lower, upper)
        pack[places["diagonal"] + k : places["diagonal"] + k + 1, :] = jnp.sum(
            jnp.where(rows == cols, upper, 0.0), axis=0, keepdims=True
        )
    for i, j in OFF_DIAGONAL:
        height = EDGES[i + 1] - EDGES[i]
        pack[places[i, j] : places[i, j] + height, :] = block(i, j)[:height]
    lane = lax.broadcasted_iota(jnp.int32, (BANDS, LANES), 1)
    mean_row = product(
        jnp.ones((8, LANES), jnp.float32), jnp.where(lane == 0, mean, 0.0), 1, 1
    )
    which = lax.broadcasted_iota(jnp.int32, (tiles, BLOCK), 0)
    for c in range(4):
        width = EDGES[c + 1] - EDGES[c]
        place = places["means"] + c * tiles
        pack[place : place + tiles, 0:width] = jnp.where(
            which[:, :width] == tile, mean_row[0:1, EDGES[c] : EDGES[c + 1]], 0.0
        )
    keep_ref[...] = pack[pl.ds(pl.multiple_of(line * half, 8), half), :]
    send_ref[...] = pack[pl.ds(pl.multiple_of((1 - line) * half, 8), half), :]


def wavelet_kernel(x_ref, other_ref, mean_ref, line_ref, samp_ref, *rest):
    own_ref, sends, (xs, matrix) = rest[0], rest[1:5], rest[5:]
    per_row = LD * SD // LANES
    mean = mean_ref[...]
    for k, ref in enumerate((x_ref, other_ref)):
        for c in range(per_row):
            at = (k * per_row + c) * LANES
            xs[:, at : at + LANES] = ref[pl.ds(c, BANDS, stride=per_row), :] - mean

    def columns(start, width):
        samp = samp_ref[:, start : start + width]
        for line in range(2 * LD):
            matrix[line * SD : (line + 1) * SD, 0:width] = (
                samp * line_ref[line : line + 1, start : start + width]
            )
        return product(xs[...], matrix[:, 0:width], 1, 0)

    for start in (0, 256):
        own_ref[:, start : start + 256] = columns(start, 256)
    start = own_ref.shape[1]
    for ref in sends:
        width = ref.shape[1]
        lane = lax.broadcasted_iota(jnp.int32, (BANDS, width), 1)
        wide = jnp.broadcast_to(mean[:, 0:1], (BANDS, width))
        ref[...] = jnp.where(lane == width - 1, wide, columns(start, width))
        start += width


def reciprocal(value):
    guess = pl.reciprocal(value, approx=True)
    return guess * (2.0 - value * guess)


def spread(value):
    return jnp.broadcast_to(value, (8, LANES))


def inverse_factor(groups):
    rows = list(groups)
    lane = lax.broadcasted_iota(jnp.int32, (8, LANES), 1)
    sub = lax.broadcasted_iota(jnp.int32, (8, LANES), 0)
    done = []
    for b in range(len(rows)):
        base = 8 * b
        current = rows[b]
        cols = [spread(current[:, base + t : base + t + 1]) for t in range(8)]
        s = [[spread(cols[t][u : u + 1, :]) if u >= t else None for t in range(8)] for u in range(8)]
        inside = (lane >= base) & (lane < base + 8)
        start = jnp.where(inside, jnp.where(lane == base + sub, 1.0, 0.0), current)
        y = [spread(start[t : t + 1, :]) for t in range(8)]
        r = [None] * 8
        l = [[None] * 8 for _ in range(8)]
        for p in range(8):
            r[p] = reciprocal(s[p][p])
            for t in range(p + 1, 8):
                l[t][p] = s[t][p] * r[p]
            for t in range(p + 1, 8):
                for u in range(t, 8):
                    s[u][t] = s[u][t] - s[u][p] * l[t][p]
                y[t] = y[t] - l[t][p] * y[p]
        z = [None] * 8
        for t in range(7, -1, -1):
            z[t] = r[t] * y[t]
            for u in range(t + 1, 8):
                z[t] = z[t] - l[u][t] * z[u]
        for g in range(b + 1, len(rows)):
            old = rows[g]
            terms = [spread(old[:, base + t : base + t + 1]) * z[t] for t in range(8)]
            while len(terms) > 1:
                terms = [terms[k] + terms[k + 1] for k in range(0, len(terms), 2)]
            rows[g] = jnp.where(inside, 0.0, old) - terms[0]
        q, d = y[0], s[0][0]
        for t in range(1, 8):
            q = jnp.where(sub == t, y[t], q)
            d = jnp.where(sub == t, s[t][t], d)
        done.append(jnp.where(lane < base + 8, q * lax.rsqrt(d), 0.0))
    return done


def whiten_kernel(tiles, where_ref, mine_ref, theirs_ref, w_ref, dev_ref, pack, a):
    places, total = payload_rows(tiles)
    half = total // 2
    line = where_ref[1]
    pack[pl.ds(pl.multiple_of(line * half, 8), half), :] = mine_ref[...]
    pack[pl.ds(pl.multiple_of((1 - line) * half, 8), half), :] = theirs_ref[...]
    at = places["means"]
    means = jnp.concatenate([pack[at + c * tiles : at + (c + 1) * tiles, :] for c in range(4)], 1)
    dev = means - jnp.sum(means, axis=0, keepdims=True) / tiles
    dev_ref[...] = dev
    between = (LD * SD) * product(dev, dev, 0, 0)
    rows, cols = square_iotas()
    trace = jnp.zeros((1, BLOCK), jnp.float32)
    for k in range(2):
        packed = pack[k * BLOCK : (k + 1) * BLOCK, :]
        turned = packed.T
        diagonal = pack[places["diagonal"] + k : places["diagonal"] + k + 1, :]
        lower = jnp.where(rows >= cols, packed, turned)
        upper = jnp.where(rows < cols, packed, jnp.where(rows > cols, turned, diagonal))
        for i, full in ((2 * k, lower), (2 * k + 1, upper)):
            low, high = EDGES[i], EDGES[i + 1]
            full = full + between[i * BLOCK : (i + 1) * BLOCK, i * BLOCK : (i + 1) * BLOCK]
            trace += jnp.sum(jnp.where(rows == cols, full, 0.0), axis=0, keepdims=True)
            a[low:high, i * BLOCK : (i + 1) * BLOCK] = full[: high - low]
    for i, j in OFF_DIAGONAL:
        low, high = EDGES[i], EDGES[i + 1]
        a[low:high, j * BLOCK : (j + 1) * BLOCK] = (
            pack[places[i, j] : places[i, j] + high - low, :]
            + between[low:high, j * BLOCK : (j + 1) * BLOCK]
        )
    load = 0.01 * (jnp.sum(trace, axis=1, keepdims=True) / BANDS)
    for i in range(4):
        low, high = EDGES[i], EDGES[i + 1]
        full = a[low:high, i * BLOCK : (i + 1) * BLOCK]
        height = high - low
        a[low:high, i * BLOCK : (i + 1) * BLOCK] = full + jnp.where(
            (rows == cols)[:height], load, 0.0
        )
    w_ref[...] = jnp.zeros_like(w_ref)
    for k in range(4):
        low, high = EDGES[k], EDGES[k + 1]
        groups = [a[low + 8 * g : low + 8 * g + 8, low : low + BLOCK] for g in range((high - low) // 8)]
        m = jnp.concatenate(inverse_factor(groups), 0)[:, : high - low]
        if k:
            w_ref[low:high, :low] = product(m, w_ref[low:high, :low], 1, 0)
        w_ref[low:high, low:high] = m
        if high < BANDS:
            factor = product(a[high:, low:high], m, 1, 1)
            for j in range(k + 1, 4):
                below = factor[EDGES[j] - high :]
                a[EDGES[j] :, EDGES[j] : EDGES[j + 1]] -= product(
                    below, below[: EDGES[j + 1] - EDGES[j]], 1, 1
                )
            w_ref[high:, :high] = w_ref[high:, :high] - product(factor, w_ref[low:high, :high], 1, 0)


def output_kernel(pixels, where_ref, own_ref, mean_ref, dev_ref, w_ref, offset_ref, chosen_ref, *rest):
    arrived, (out1_ref, out2_ref, out3_ref, approx_ref), (d, small) = rest[:4], rest[4:8], rest[8:]
    tile = where_ref[0]
    count = own_ref.shape[1]
    mean = mean_ref[...]
    tiles = dev_ref.shape[0]
    which = lax.broadcasted_iota(jnp.int32, (tiles, count), 0)
    total = own_ref[...] + product(
        dev_ref[:, 0:BANDS], jnp.where(which == tile, offset_ref[4:5, :], 0.0), 0, 0
    )
    start = 0
    for k, ref in enumerate(arrived):
        width = ref.shape[1]
        lane = lax.broadcasted_iota(jnp.int32, (BANDS, width), 1)
        wide = jnp.broadcast_to(mean[:, 0:1], (BANDS, width))
        values = ref[...] - jnp.where(lane == width - 1, wide, 0.0)
        chosen = jnp.broadcast_to(chosen_ref[start : start + width, 0:1], (width, count))
        columns = lax.broadcasted_iota(jnp.int32, (width, count), 1)
        row = lax.broadcasted_iota(jnp.int32, (width, count), 0)
        select = jnp.where(row == width - 1, offset_ref[k : k + 1, :], jnp.where(chosen == columns, 1.0, 0.0))
        total += product(values, select, 1, 0)
        start += width
    d[...] = total * (float(pixels) ** 0.5)
    for k in range(4):
        low, high = EDGES[k], EDGES[k + 1]
        out = product(w_ref[low:high, :high], d[0:high, :], 1, 0)
        for sb in range(3):
            out1_ref[sb * BANDS + low : sb * BANDS + high, :] = out[:, sb * LANES : (sb + 1) * LANES]
        small[low:high, :] = out[:, 3 * LANES :]

    def repack(first, width):
        together = LANES // width
        height = BANDS // together
        lane = lax.broadcasted_iota(jnp.int32, (height, LANES), 1)
        result = jnp.zeros((height, LANES), jnp.float32)
        for k in range(together):
            taken = small[pl.ds(k, height, stride=together), :]
            moved = pltpu.roll(taken, (k * width - first) % LANES, 1)
            result = jnp.where((lane >= k * width) & (lane < (k + 1) * width), moved, result)
        return result

    size2, size3 = (LD // 4) * (SD // 4), (LD // 8) * (SD // 8)
    rows2, rows3 = BANDS * size2 // LANES, BANDS * size3 // LANES
    for sb in range(3):
        out2_ref[sb * rows2 : (sb + 1) * rows2, :] = repack(sb * size2, size2)
        out3_ref[sb * rows3 : (sb + 1) * rows3, :] = repack(3 * size2 + sb * size3, size3)
    approx_ref[...] = repack(3 * size2 + 3 * size3, size3)


def swapped(array, axis, bit):
    return lax.ppermute(array, axis, [(i, i ^ bit) for i in range(lax.axis_size(axis))])


def shifted(array, axis, step):
    count = lax.axis_size(axis)
    return lax.ppermute(array, axis, [(i, i + step) for i in range(count) if 0 <= i + step < count])


VMEM = pl.BlockSpec(memory_space=pltpu.VMEM)
SMEM = pl.BlockSpec(memory_space=pltpu.SMEM)


def call(kernel, shapes, inputs, scratch, flops):
    specs = [SMEM if value.dtype == jnp.int32 and value.ndim == 1 else VMEM for value in inputs]
    size = sum(value.size * 4 for value in inputs)
    return pl.pallas_call(
        kernel,
        out_shape=[jax.ShapeDtypeStruct(shape, jnp.float32) for shape in shapes],
        in_specs=specs,
        out_specs=[VMEM] * len(shapes),
        scratch_shapes=[pltpu.VMEM(shape, jnp.float32) for shape in scratch],
        compiler_params=pltpu.CompilerParams(vmem_limit_bytes=40 * 2**20),
        cost_estimate=pl.CostEstimate(flops=flops, bytes_accessed=size, transcendentals=0),
    )(*inputs)


def local(constants, cube):
    line_table, samp_table, chosen, offset_table = constants
    n_samp, n_line = lax.axis_size("samp"), lax.axis_size("line")
    tiles = n_samp * n_line
    samp, line = lax.axis_index("samp"), lax.axis_index("line")
    where = jnp.stack([samp * n_line + line, line]).astype(jnp.int32)
    count = LD * SD
    x = cube.reshape(BANDS * count // LANES, LANES)
    other = swapped(x, "line", 1)
    _, total = payload_rows(tiles)
    half = total // 2
    send, keep, mean = call(
        functools.partial(gram_kernel, tiles),
        [(half, LANES), (half, LANES), (BANDS, LANES)],
        [where, x],
        [(4 * BLOCK, count), (total, LANES)],
        2 * BANDS * BANDS * count * 4,
    )
    summed = keep + swapped(send, "line", 1)
    bit = samp & 1
    quarter = half // 2
    kept = lax.dynamic_slice_in_dim(summed, bit * quarter, quarter, 0)
    given = lax.dynamic_slice_in_dim(summed, (1 - bit) * quarter, quarter, 0)
    kept = kept + swapped(given, "samp", 1)
    step = 2
    while step < n_samp:
        kept = kept + swapped(kept, "samp", step)
        step *= 2
    back = swapped(kept, "samp", 1)
    mine = jnp.where(bit == 0, jnp.concatenate([kept, back]), jnp.concatenate([back, kept]))
    theirs = swapped(mine, "line", 1)

    own, *sends = call(
        wavelet_kernel,
        [(BANDS, count)] + [(BANDS, width) for _, width in SENDS],
        [x, other, mean, jnp.asarray(line_table)[line], jnp.asarray(samp_table)[samp]],
        [(BANDS, 2 * count), (2 * count, 256)],
        2 * BANDS * 2 * count * line_table.shape[2] * 6,
    )
    arrived = [shifted(value, "samp", step) for value, (step, _) in zip(sends, SENDS)]

    w, dev = call(
        functools.partial(whiten_kernel, tiles),
        [(BANDS, BANDS), (tiles, 4 * BLOCK)],
        [where, mine, theirs],
        [(total, LANES), (BANDS, 4 * BLOCK)],
        2 * 10**10,
    )
    outs = call(
        functools.partial(output_kernel, count * tiles),
        [
            (3 * BANDS * (count // 4) // LANES, LANES),
            (3 * BANDS * (count // 16) // LANES, LANES),
            (3 * BANDS * (count // 64) // LANES, LANES),
            (BANDS * (count // 64) // LANES, LANES),
        ],
        [where, own, mean, dev, w, jnp.asarray(offset_table)[samp, line], jnp.asarray(chosen)] + arrived,
        [(BANDS, count), (BANDS, LANES)],
        2 * BANDS * BANDS * count * 6,
    )
    return tuple(out.reshape(-1) for out in outs)


def solution(mesh):
    n_samp, n_line = mesh.shape["samp"], mesh.shape["line"]
    assert n_line == 2 and n_samp & (n_samp - 1) == 0
    constants = build_constants(n_samp, n_line)
    spec = P(("groups", "samp", "line"))
    return jax.shard_map(
        functools.partial(local, constants),
        mesh=mesh,
        in_specs=(spec,),
        out_specs=(spec,) * 4,
        check_vma=False,
    )
```

profile of v0, /device:TPU:0, one launch (start us, length us, event | category | flops | bytes accessed | tf_op | source)
XLA Modules:
  0.0 83.0 jit_solution(6837203047844148592)
XLA Ops:
  0.6 0.1 pad_add_fusion.where_ref
  0.7 1.2 %copy-done = f32[221184]{0:T(1024)S(1)} copy-done((f32[221184]{0:T(1024)S(1)}, f32[221184]{0:T(1024)}, u32[]{:S(2)}) %copy-start) | copy-done | bytes 884760
  1.9 3.1 %shard_map.84 = (f32[432,128]{1,0:T(8,128)S(1)}, f32[432,128]{1,0:T(8,128)S(1)}, f32[432,128]{1,0:T(8,128)S(1)}) custom-call(s32[2]{0:T(128)S(1)} %pad_add_fusion.where_ref, f32[1728,128]{1,0:T(8,128)S(1)} %bitcast.13), custom_call_target="tpu_custom_call" | custom-call | flops 764411904 | bytes 884744 | tf_op jit(solution)/shard_map/pallas_call | solution.py:402
  5.0 0.0 copy-start.1
  5.0 0.5 collective-permute-start.1
  5.5 1.1 %collective-permute-done.1 = f32[432,128]{1,0:T(8,128)S(1)} collective-permute-done((f32[432,128]{1,0:T(8,128)S(1)}, f32[432,128]{1,0:T(8,128)S(1)}, u32[]{:S(2)}, u32[]{:S(2)}) %collective-permute-start.1) | collective-permute-done | bytes 221216 | tf_op jit(solution)/shard_map/ppermute | solution.py:387
  6.7 3.0 %collective-permute-start.2 = (f32[216,128]{1,0:T(8,128)S(1)}, f32[216,128]{1,0:T(8,128)S(1)}, u32[]{:S(2)}, u32[]{:S(2)}) collective-permute-start(f32[216,128]{1,0:T(8,128)S(1)} %constant_dynamic-slice_fusion), channel_id=1, source_target_pairs={{0,2},{2,0},{4,6},{6,4},{8,10},{10,8},{12,14},{14,12},{1,3},{3,1},... | collective-permute-start | bytes 331784 | tf_op jit(solution)/shard_map/ppermute | solution.py:387
  9.7 0.0 collective-permute-start
  9.7 3.4 %collective-permute-done.2 = f32[216,128]{1,0:T(8,128)S(1)} collective-permute-done((f32[216,128]{1,0:T(8,128)S(1)}, f32[216,128]{1,0:T(8,128)S(1)}, u32[]{:S(2)}, u32[]{:S(2)}) %collective-permute-start.2) | collective-permute-done | bytes 110624 | tf_op jit(solution)/shard_map/ppermute | solution.py:387
  13.0 1.9 %collective-permute-start.3 = (f32[216,128]{1,0:T(8,128)S(1)}, f32[216,128]{1,0:T(8,128)S(1)}, u32[]{:S(2)}, u32[]{:S(2)}) collective-permute-start(f32[216,128]{1,0:T(8,128)S(1)} %dynamic-slice_add_fusion), channel_id=1, source_target_pairs={{0,4},{2,6},{4,0},{6,2},{8,12},{10,14},{12,8},{14,10},{1,5},{3,7},... | collective-permute-start | bytes 331784 | tf_op jit(solution)/shard_map/ppermute | solution.py:387
  14.9 2.9 %collective-permute-done.3 = f32[216,128]{1,0:T(8,128)S(1)} collective-permute-done((f32[216,128]{1,0:T(8,128)S(1)}, f32[216,128]{1,0:T(8,128)S(1)}, u32[]{:S(2)}, u32[]{:S(2)}) %collective-permute-start.3) | collective-permute-done | bytes 110624 | tf_op jit(solution)/shard_map/ppermute | solution.py:387
  17.9 2.9 %collective-permute-start.4 = (f32[216,128]{1,0:T(8,128)S(1)}, f32[216,128]{1,0:T(8,128)S(1)}, u32[]{:S(2)}, u32[]{:S(2)}) collective-permute-start(f32[216,128]{1,0:T(8,128)S(1)} %add.36), channel_id=1, source_target_pairs={{0,8},{2,10},{4,12},{6,14},{8,0},{10,2},{12,4},{14,6},{1,9},{3,11}... | collective-permute-start | bytes 331784 | tf_op jit(solution)/shard_map/ppermute | solution.py:387
  20.7 0.9 %dynamic-slice_bitcast_fusion.1.samp_ref = f32[16,1280]{1,0:T(8,128)S(1)} fusion(f32[8,16,1280]{2,1,0:T(8,128)} %constant.29.clone, s32[]{:T(128)S(6)} %select_n.23), kind=kLoop, calls=%fused_computation.3 | loop fusion | bytes 163844 | tf_op jit(solution)/shard_map/squeeze | solution.py:448
  21.6 1.9 %collective-permute-done.4 = f32[216,128]{1,0:T(8,128)S(1)} collective-permute-done((f32[216,128]{1,0:T(8,128)S(1)}, f32[216,128]{1,0:T(8,128)S(1)}, u32[]{:S(2)}, u32[]{:S(2)}) %collective-permute-start.4) | collective-permute-done | bytes 110624 | tf_op jit(solution)/shard_map/ppermute | solution.py:387
  23.6 3.0 %collective-permute-start.5 = (f32[216,128]{1,0:T(8,128)S(1)}, f32[216,128]{1,0:T(8,128)S(1)}, u32[]{:S(2)}, u32[]{:S(2)}) collective-permute-start(f32[216,128]{1,0:T(8,128)S(1)} %add.37), channel_id=1, source_target_pairs={{0,2},{2,0},{4,6},{6,4},{8,10},{10,8},{12,14},{14,12},{1,3},{3,1},... | collective-permute-start | bytes 331784 | tf_op jit(solution)/shard_map/ppermute | solution.py:387
  26.6 0.7 dynamic-slice_bitcast_fusion.2.offset_ref
  27.3 2.0 %collective-permute-done.5 = f32[216,128]{1,0:T(8,128)S(1)} collective-permute-done((f32[216,128]{1,0:T(8,128)S(1)}, f32[216,128]{1,0:T(8,128)S(1)}, u32[]{:S(2)}, u32[]{:S(2)}) %collective-permute-start.5) | collective-permute-done | bytes 110624 | tf_op jit(solution)/shard_map/ppermute | solution.py:387
  29.3 0.1 collective-permute-start.6
  29.4 0.0 collective-permute-done.other_ref
  29.4 8.6 %shard_map.85 = (f32[432,512]{1,0:T(8,128)S(1)}, f32[432,256]{1,0:T(8,128)S(1)}, f32[432,256]{1,0:T(8,128)S(1)}, f32[432,128]{1,0:T(8,128)S(1)}, f32[432,128]{1,0:T(8,128)S(1)}) custom-call(f32[1728,128]{1,0:T(8,128)S(1)} %bitcast.15, f32[1728,128]{1,0:T(8,128)S(1)} %collective-permute-done.other_ref, f32[432,128]{1,0:T(8,128)S(1)} %get-tuple-element.18.mean_ref, ...), custom_call_target="tpu_custom_call" | custom-call | flops 6794772480 | bytes 2400256 | tf_op jit(solution)/shard_map/pallas_call | solution.py:402
  38.0 1.3 %collective-permute-start.7 = (f32[432,256]{1,0:T(8,128)S(1)}, f32[432,256]{1,0:T(8,128)S(1)}, u32[]{:S(2)}, u32[]{:S(2)}) collective-permute-start(f32[432,256]{1,0:T(8,128)S(1)} %get-tuple-element.24), channel_id=1, source_target_pairs={{2,0},{4,2},{6,4},{8,6},{10,8},{12,10},{14,12},{3,1},{5,3},{7,5},{... | collective-permute-start | bytes 1327112 | tf_op jit(solution)/shard_map/ppermute | solution.py:392
  39.3 4.6 %collective-permute-start.8 = (f32[432,256]{1,0:T(8,128)S(1)}, f32[432,256]{1,0:T(8,128)S(1)}, u32[]{:S(2)}, u32[]{:S(2)}) collective-permute-start(f32[432,256]{1,0:T(8,128)S(1)} %get-tuple-element.25), channel_id=1, source_target_pairs={{0,2},{2,4},{4,6},{6,8},{8,10},{10,12},{12,14},{1,3},{3,5},{5,7},{... | collective-permute-start | bytes 1327112 | tf_op jit(solution)/shard_map/ppermute | solution.py:392
  43.9 1.3 %collective-permute-start.9 = (f32[432,128]{1,0:T(8,128)S(1)}, f32[432,128]{1,0:T(8,128)S(1)}, u32[]{:S(2)}, u32[]{:S(2)}) collective-permute-start(f32[432,128]{1,0:T(8,128)S(1)} %get-tuple-element.26), channel_id=1, source_target_pairs={{4,0},{6,2},{8,4},{10,6},{12,8},{14,10},{5,1},{7,3},{9,5},{11,7},{... | collective-permute-start | bytes 663560 | tf_op jit(solution)/shard_map/ppermute | solution.py:392
  45.2 0.0 copy-start.2
  45.2 4.9 %collective-permute-start.10 = (f32[432,128]{1,0:T(8,128)S(1)}, f32[432,128]{1,0:T(8,128)S(1)}, u32[]{:S(2)}, u32[]{:S(2)}) collective-permute-start(f32[432,128]{1,0:T(8,128)S(1)} %get-tuple-element.27), channel_id=1, source_target_pairs={{0,4},{2,6},{4,8},{6,10},{8,12},{10,14},{1,5},{3,7},{5,9},{7,11},{... | collective-permute-start | bytes 663560 | tf_op jit(solution)/shard_map/ppermute | solution.py:392
  50.1 0.0 collective-permute-done.6.theirs_ref
  50.1 26.1 %shard_map.86 = (f32[432,432]{1,0:T(8,128)S(1)}, f32[16,512]{1,0:T(8,128)S(1)}) custom-call(s32[2]{0:T(128)S(1)} %pad_add_fusion.where_ref, f32[432,128]{1,0:T(8,128)S(1)} %maximum_select_fusion.mine_ref, f32[432,128]{1,0:T(8,128)S(1)} %collective-permute-done.6.theirs_ref), custom_call_target="tpu_custom_call" | custom-call | flops 20000000000 | bytes 442376 | tf_op jit(solution)/shard_map/pallas_call | solution.py:402
  76.2 0.0 collective-permute-done.9.rest_2_
  76.2 0.0 collective-permute-done.10.rest_3_
  76.2 0.0 collective-permute-done.7.rest_0_
  76.3 0.0 collective-permute-done.8.rest_1_
  76.3 6.8 %shard_map.87 = (f32[1296,128]{1,0:T(8,128)}, f32[324,128]{1,0:T(8,128)}, f32[81,128]{1,0:T(8,128)}, f32[27,128]{1,0:T(8,128)}) custom-call(s32[2]{0:T(128)S(1)} %pad_add_fusion.where_ref, f32[432,512]{1,0:T(8,128)S(1)} %get-tuple-element.19.own_ref, f32[432,128]{1,0:T(8,128)S(1)} %get-tuple-element.18.mean_ref, f32[16,512]{1,0:T(8,128)S(1)} %get-tuple-element.22.dev_ref, ...), custom_call_target="tpu_custom_call" | custom-call | flops 1146617856 | bytes 3621896 | tf_op jit(solution)/shard_map/pallas_call | solution.py:402
  (12 shorter events, 0.1 us)
Async XLA Ops:
  0.7 1.2 %copy-start = (f32[221184]{0:T(1024)S(1)}, f32[221184]{0:T(1024)}, u32[]{:S(2)}) copy-start(f32[221184]{0:T(1024)} %param.5) | copy-start | bytes 2654212
  1.9 13.0 %copy-start.3 = (f32[2,64,1280]{2,1,0:T(8,128)S(1)}, f32[2,64,1280]{2,1,0:T(8,128)}, u32[]{:S(2)}) copy-start(f32[2,64,1280]{2,1,0:T(8,128)} %constant.28.clone) | copy-start | bytes 1966084
  5.0 4.6 %copy-start.1 = (f32[221184]{0:T(1024)S(1)}, f32[221184]{0:T(1024)}, u32[]{:S(2)}) copy-start(f32[221184]{0:T(1024)} %param.5) | copy-start | bytes 2654212
  5.0 1.6 %collective-permute-start.1 = (f32[432,128]{1,0:T(8,128)S(1)}, f32[432,128]{1,0:T(8,128)S(1)}, u32[]{:S(2)}, u32[]{:S(2)}) collective-permute-start(f32[432,128]{1,0:T(8,128)S(1)} %get-tuple-element.21), channel_id=1, source_target_pairs={{0,1},{1,0},{2,3},{3,2},{4,5},{5,4},{6,7},{7,6},{8,9},{9,8},{10,11... | collective-permute-start | bytes 663560 | tf_op jit(solution)/shard_map/ppermute | solution.py:387
  6.7 6.3 %collective-permute-start.2 = (f32[216,128]{1,0:T(8,128)S(1)}, f32[216,128]{1,0:T(8,128)S(1)}, u32[]{:S(2)}, u32[]{:S(2)}) collective-permute-start(f32[216,128]{1,0:T(8,128)S(1)} %constant_dynamic-slice_fusion), channel_id=1, source_target_pairs={{0,2},{2,0},{4,6},{6,4},{8,10},{10,8},{12,14},{14,12},{1,3},{3,1},... | collective-permute-start | bytes 331784 | tf_op jit(solution)/shard_map/ppermute | solution.py:387
  9.7 19.8 %collective-permute-start = (f32[1728,128]{1,0:T(8,128)S(1)}, f32[1728,128]{1,0:T(8,128)S(1)}, u32[]{:S(2)}, u32[]{:S(2)}) collective-permute-start(f32[1728,128]{1,0:T(8,128)S(1)} %bitcast.14), channel_id=1, source_target_pairs={{0,1},{1,0},{2,3},{3,2},{4,5},{5,4},{6,7},{7,6},{8,9},{9,8},{10,11... | collective-permute-start | bytes 2654216 | tf_op jit(solution)/shard_map/ppermute | solution.py:387
  13.0 4.8 %collective-permute-start.3 = (f32[216,128]{1,0:T(8,128)S(1)}, f32[216,128]{1,0:T(8,128)S(1)}, u32[]{:S(2)}, u32[]{:S(2)}) collective-permute-start(f32[216,128]{1,0:T(8,128)S(1)} %dynamic-slice_add_fusion), channel_id=1, source_target_pairs={{0,4},{2,6},{4,0},{6,2},{8,12},{10,14},{12,8},{14,10},{1,5},{3,7},... | collective-permute-start | bytes 331784 | tf_op jit(solution)/shard_map/ppermute | solution.py:387
  17.9 5.7 %collective-permute-start.4 = (f32[216,128]{1,0:T(8,128)S(1)}, f32[216,128]{1,0:T(8,128)S(1)}, u32[]{:S(2)}, u32[]{:S(2)}) collective-permute-start(f32[216,128]{1,0:T(8,128)S(1)} %add.36), channel_id=1, source_target_pairs={{0,8},{2,10},{4,12},{6,14},{8,0},{10,2},{12,4},{14,6},{1,9},{3,11}... | collective-permute-start | bytes 331784 | tf_op jit(solution)/shard_map/ppermute | solution.py:387
  23.6 5.7 %collective-permute-start.5 = (f32[216,128]{1,0:T(8,128)S(1)}, f32[216,128]{1,0:T(8,128)S(1)}, u32[]{:S(2)}, u32[]{:S(2)}) collective-permute-start(f32[216,128]{1,0:T(8,128)S(1)} %add.37), channel_id=1, source_target_pairs={{0,2},{2,0},{4,6},{6,4},{8,10},{10,8},{12,14},{14,12},{1,3},{3,1},... | collective-permute-start | bytes 331784 | tf_op jit(solution)/shard_map/ppermute | solution.py:387
  29.3 20.8 %collective-permute-start.6 = (f32[432,128]{1,0:T(8,128)S(1)}, f32[432,128]{1,0:T(8,128)S(1)}, u32[]{:S(2)}, u32[]{:S(2)}) collective-permute-start(f32[432,128]{1,0:T(8,128)S(1)} %maximum_select_fusion.mine_ref), channel_id=1, source_target_pairs={{0,1},{1,0},{2,3},{3,2},{4,5},{5,4},{6,7},{7,6},{8,9},{9,8},{10,11... | collective-permute-start | bytes 663560 | tf_op jit(solution)/shard_map/ppermute | solution.py:387
  38.0 38.2 %collective-permute-start.7 = (f32[432,256]{1,0:T(8,128)S(1)}, f32[432,256]{1,0:T(8,128)S(1)}, u32[]{:S(2)}, u32[]{:S(2)}) collective-permute-start(f32[432,256]{1,0:T(8,128)S(1)} %get-tuple-element.24), channel_id=1, source_target_pairs={{2,0},{4,2},{6,4},{8,6},{10,8},{12,10},{14,12},{3,1},{5,3},{7,5},{... | collective-permute-start | bytes 1327112 | tf_op jit(solution)/shard_map/ppermute | solution.py:392
  39.3 36.9 %collective-permute-start.8 = (f32[432,256]{1,0:T(8,128)S(1)}, f32[432,256]{1,0:T(8,128)S(1)}, u32[]{:S(2)}, u32[]{:S(2)}) collective-permute-start(f32[432,256]{1,0:T(8,128)S(1)} %get-tuple-element.25), channel_id=1, source_target_pairs={{0,2},{2,4},{4,6},{6,8},{8,10},{10,12},{12,14},{1,3},{3,5},{5,7},{... | collective-permute-start | bytes 1327112 | tf_op jit(solution)/shard_map/ppermute | solution.py:392
  43.9 32.3 %collective-permute-start.9 = (f32[432,128]{1,0:T(8,128)S(1)}, f32[432,128]{1,0:T(8,128)S(1)}, u32[]{:S(2)}, u32[]{:S(2)}) collective-permute-start(f32[432,128]{1,0:T(8,128)S(1)} %get-tuple-element.26), channel_id=1, source_target_pairs={{4,0},{6,2},{8,4},{10,6},{12,8},{14,10},{5,1},{7,3},{9,5},{11,7},{... | collective-permute-start | bytes 663560 | tf_op jit(solution)/shard_map/ppermute | solution.py:392
  45.2 31.1 %copy-start.2 = (s32[768,128]{1,0:T(8,128)S(1)}, s32[768,128]{1,0:T(8,128)}, u32[]{:S(2)}) copy-start(s32[768,128]{1,0:T(8,128)} %constant.31.clone.chosen_ref) | copy-start | bytes 1179652
  45.2 31.0 %collective-permute-start.10 = (f32[432,128]{1,0:T(8,128)S(1)}, f32[432,128]{1,0:T(8,128)S(1)}, u32[]{:S(2)}, u32[]{:S(2)}) collective-permute-start(f32[432,128]{1,0:T(8,128)S(1)} %get-tuple-element.27), channel_id=1, source_target_pairs={{0,4},{2,6},{4,8},{6,10},{8,12},{10,14},{1,5},{3,7},{5,9},{7,11},{... | collective-permute-start | bytes 663560 | tf_op jit(solution)/shard_map/ppermute | solution.py:392
where the time goes:
time: 83.4 us; the launch traced here: 83 us
  Pallas kernels  44.6 us (53%)
  starting transfers between devices  23.3 us (28%)
  waiting for transfers between devices  11.4 us (14%)
  local copies, waits for them, and re-layouts  2.83 us (3%)
    pallas_call x4, Pallas kernels, call(): pl.pallas_call(kernel, out_shape=[jax.ShapeDtypeStruct(shape, jnp.float32...  44.6 us
    ppermute x4, starting transfers between devices, shifted(): lax.ppermute(array, axis, [(i, i + step) for i in range(count) if 0 <= i...  12 us
    ppermute x7, waiting for transfers between devices, swapped(): lax.ppermute(array, axis, [(i, i ^ bit) for i in range(lax.axis_size(axis...  11.3 us
    ppermute x7, starting transfers between devices, swapped(): lax.ppermute(array, axis, [(i, i ^ bit) for i in range(lax.axis_size(axis...  11.3 us
  transfers between devices with their start and end apart: 11, of which 5 were waited for; matrix products, arithmetic and copies ran while one was open for 2% of the time, Pallas kernels for 42%

commit v1 on v0

--- a/solution.py
+++ b/solution.py
@@ -227,49 +227,78 @@
         start += width
 
 
-def reciprocal(value):
-    guess = pl.reciprocal(value, approx=True)
-    return guess * (2.0 - value * guess)
-
-
 def spread(value):
     return jnp.broadcast_to(value, (8, LANES))
 
 
-def inverse_factor(groups):
+def added(terms):
+    terms = list(terms)
+    while len(terms) > 1:
+        terms = [sum(terms[k + 1 : k + 2], terms[k]) for k in range(0, len(terms), 2)]
+    return terms[0]
+
+
+NEAR = 2
+
+
+def inverse_factor(groups, held):
     rows = list(groups)
     lane = lax.broadcasted_iota(jnp.int32, (8, LANES), 1)
     sub = lax.broadcasted_iota(jnp.int32, (8, LANES), 0)
     done = []
+
+    def columns(group, base):
+        return [spread(group[:, base + t : base + t + 1]) for t in range(8)]
+
+    following = columns(rows[0], 0)
     for b in range(len(rows)):
-        base = 8 * b
+        base, slot = 8 * b, b % 2
         current = rows[b]
-        cols = [spread(current[:, base + t : base + t + 1]) for t in range(8)]
-        s = [[spread(cols[t][u : u + 1, :]) if u >= t else None for t in range(8)] for u in range(8)]
+        for t in range(8):
+            held[slot, t] = following[t]
+        s = [[spread(held[slot, t, u : u + 1, :]) if u >= t else None for t in range(8)] for u in range(8)]
         inside = (lane >= base) & (lane < base + 8)
         start = jnp.where(inside, jnp.where(lane == base + sub, 1.0, 0.0), current)
         y = [spread(start[t : t + 1, :]) for t in range(8)]
+        near = list(range(b + 1, min(len(rows), b + 1 + NEAR)))
+        far = list(range(b + 1 + NEAR, len(rows)))
+        g = {i: columns(rows[i], base) for i in near}
+        if near:
+            raw = columns(rows[b + 1], base + 8)
         r = [None] * 8
         l = [[None] * 8 for _ in range(8)]
         for p in range(8):
-            r[p] = reciprocal(s[p][p])
+            r[p] = pl.reciprocal(s[p][p], approx=True)
             for t in range(p + 1, 8):
                 l[t][p] = s[t][p] * r[p]
             for t in range(p + 1, 8):
                 for u in range(t, 8):
-                    s[u][t] = s[u][t] - s[u][p] * l[t][p]
+                    if u == t == p + 1:
+                        s[u][t] = s[u][t] - (s[u][p] * s[t][p]) * r[p]
+                    else:
+                        s[u][t] = s[u][t] - s[u][p] * l[t][p]
+                for i in near:
+                    g[i][t] = g[i][t] - g[i][p] * l[t][p]
                 y[t] = y[t] - l[t][p] * y[p]
-        z = [None] * 8
-        for t in range(7, -1, -1):
-            z[t] = r[t] * y[t]
-            for u in range(t + 1, 8):
-                z[t] = z[t] - l[u][t] * z[u]
-        for g in range(b + 1, len(rows)):
-            old = rows[g]
-            terms = [spread(old[:, base + t : base + t + 1]) * z[t] for t in range(8)]
-            while len(terms) > 1:
-                terms = [terms[k] + terms[k + 1] for k in range(0, len(terms), 2)]
-            rows[g] = jnp.where(inside, 0.0, old) - terms[0]
+        scaled = {i: [g[i][p] * r[p] for p in range(8)] for i in near}
+        if near:
+            for p in range(8):
+                held[slot, 8 + p] = scaled[b + 1][p]
+            following = [
+                raw[t] - added(g[b + 1][p] * spread(held[slot, 8 + p, t : t + 1, :]) for p in range(8))
+                for t in range(8)
+            ]
+        for i in near:
+            rows[i] = jnp.where(inside, 0.0, rows[i]) - added(scaled[i][p] * y[p] for p in range(8))
+        if far:
+            z = [None] * 8
+            for t in range(7, -1, -1):
+                z[t] = r[t] * y[t]
+                for u in range(t + 1, 8):
+                    z[t] = z[t] - l[u][t] * z[u]
+            for i in far:
+                old = columns(rows[i], base)
+                rows[i] = jnp.where(inside, 0.0, rows[i]) - added(old[t] * z[t] for t in range(8))
         q, d = y[0], s[0][0]
         for t in range(1, 8):
             q = jnp.where(sub == t, y[t], q)
@@ -278,7 +307,7 @@
     return done
 
 
-def whiten_kernel(tiles, where_ref, mine_ref, theirs_ref, w_ref, dev_ref, pack, a):
+def whiten_kernel(tiles, where_ref, mine_ref, theirs_ref, w_ref, dev_ref, pack, a, held):
     places, total = payload_rows(tiles)
     half = total // 2
     line = where_ref[1]
@@ -320,7 +349,7 @@
     for k in range(4):
         low, high = EDGES[k], EDGES[k + 1]
         groups = [a[low + 8 * g : low + 8 * g + 8, low : low + BLOCK] for g in range((high - low) // 8)]
-        m = jnp.concatenate(inverse_factor(groups), 0)[:, : high - low]
+        m = jnp.concatenate(inverse_factor(groups, held), 0)[:, : high - low]
         if k:
             w_ref[low:high, :low] = product(m, w_ref[low:high, :low], 1, 0)
         w_ref[low:high, low:high] = m
@@ -455,7 +484,7 @@
         functools.partial(whiten_kernel, tiles),
         [(BANDS, BANDS), (tiles, 4 * BLOCK)],
         [where, mine, theirs],
-        [(total, LANES), (BANDS, 4 * BLOCK)],
+        [(total, LANES), (BANDS, 4 * BLOCK), (2, 16, 8, LANES)],
         2 * 10**10,
     )
     outs = call(

time: 83.4 us -> 70 us (0.84)
  Pallas kernels: 44.6 us -> 31.2 us
    pallas_call x4, Pallas kernels: 44.6 us -> 31.2 us  [call(): pl.pallas_call(kernel, out_shape=[jax.ShapeDtypeStruct(shape, jnp.float32...]
  transfers between devices with their start and end apart: 11 -> 11, of which waited for: 5 -> 5; matrix products, arithmetic and copies ran while one was open for 2% -> 2% of each run, Pallas kernels for 42% -> 30%
where the time goes in v1:
time: 70 us; the launch traced here: 69.7 us
  Pallas kernels  31.2 us (45%)
  starting transfers between devices  23.3 us (33%)
  waiting for transfers between devices  11.4 us (16%)
  local copies, waits for them, and re-layouts  2.83 us (4%)
  between operations  0.8 us (1%)
    pallas_call x4, Pallas kernels, call(): pl.pallas_call(kernel, out_shape=[jax.ShapeDtypeStruct(shape, jnp.float32...  31.2 us
    ppermute x4, starting transfers between devices, shifted(): lax.ppermute(array, axis, [(i, i + step) for i in range(count) if 0 <= i...  12 us
    ppermute x7, waiting for transfers between devices, swapped(): lax.ppermute(array, axis, [(i, i ^ bit) for i in range(lax.axis_size(axis...  11.3 us
    ppermute x7, starting transfers between devices, swapped(): lax.ppermute(array, axis, [(i, i ^ bit) for i in range(lax.axis_size(axis...  11.3 us
  transfers between devices with their start and end apart: 11, of which 5 were waited for; matrix products, arithmetic and copies ran while one was open for 2% of the time, Pallas kernels for 30%

profile of v1, /device:TPU:0, one launch (start us, length us, event | category | flops | bytes accessed | tf_op | source)
XLA Modules:
  0.0 69.7 jit_solution(11202307178671963557)
XLA Ops:
  0.6 0.1 pad_add_fusion.where_ref
  0.7 1.2 %copy-done = f32[221184]{0:T(1024)S(1)} copy-done((f32[221184]{0:T(1024)S(1)}, f32[221184]{0:T(1024)}, u32[]{:S(2)}) %copy-start) | copy-done | bytes 884760
  1.9 3.1 %shard_map.84 = (f32[432,128]{1,0:T(8,128)S(1)}, f32[432,128]{1,0:T(8,128)S(1)}, f32[432,128]{1,0:T(8,128)S(1)}) custom-call(s32[2]{0:T(128)S(1)} %pad_add_fusion.where_ref, f32[1728,128]{1,0:T(8,128)S(1)} %bitcast.13), custom_call_target="tpu_custom_call" | custom-call | flops 764411904 | bytes 884744 | tf_op jit(solution)/shard_map/pallas_call | solution.py:431
  5.0 0.0 copy-start.1
  5.0 0.5 collective-permute-start.1
  5.5 1.1 %collective-permute-done.1 = f32[432,128]{1,0:T(8,128)S(1)} collective-permute-done((f32[432,128]{1,0:T(8,128)S(1)}, f32[432,128]{1,0:T(8,128)S(1)}, u32[]{:S(2)}, u32[]{:S(2)}) %collective-permute-start.1) | collective-permute-done | bytes 221216 | tf_op jit(solution)/shard_map/ppermute | solution.py:416
  6.7 3.0 %collective-permute-start.2 = (f32[216,128]{1,0:T(8,128)S(1)}, f32[216,128]{1,0:T(8,128)S(1)}, u32[]{:S(2)}, u32[]{:S(2)}) collective-permute-start(f32[216,128]{1,0:T(8,128)S(1)} %constant_dynamic-slice_fusion), channel_id=1, source_target_pairs={{0,2},{2,0},{4,6},{6,4},{8,10},{10,8},{12,14},{14,12},{1,3},{3,1},... | collective-permute-start | bytes 331784 | tf_op jit(solution)/shard_map/ppermute | solution.py:416
  9.7 0.0 collective-permute-start
  9.7 3.4 %collective-permute-done.2 = f32[216,128]{1,0:T(8,128)S(1)} collective-permute-done((f32[216,128]{1,0:T(8,128)S(1)}, f32[216,128]{1,0:T(8,128)S(1)}, u32[]{:S(2)}, u32[]{:S(2)}) %collective-permute-start.2) | collective-permute-done | bytes 110624 | tf_op jit(solution)/shard_map/ppermute | solution.py:416
  13.0 1.9 %collective-permute-start.3 = (f32[216,128]{1,0:T(8,128)S(1)}, f32[216,128]{1,0:T(8,128)S(1)}, u32[]{:S(2)}, u32[]{:S(2)}) collective-permute-start(f32[216,128]{1,0:T(8,128)S(1)} %dynamic-slice_add_fusion), channel_id=1, source_target_pairs={{0,4},{2,6},{4,0},{6,2},{8,12},{10,14},{12,8},{14,10},{1,5},{3,7},... | collective-permute-start | bytes 331784 | tf_op jit(solution)/shard_map/ppermute | solution.py:416
  14.9 2.9 %collective-permute-done.3 = f32[216,128]{1,0:T(8,128)S(1)} collective-permute-done((f32[216,128]{1,0:T(8,128)S(1)}, f32[216,128]{1,0:T(8,128)S(1)}, u32[]{:S(2)}, u32[]{:S(2)}) %collective-permute-start.3) | collective-permute-done | bytes 110624 | tf_op jit(solution)/shard_map/ppermute | solution.py:416
  17.9 2.9 %collective-permute-start.4 = (f32[216,128]{1,0:T(8,128)S(1)}, f32[216,128]{1,0:T(8,128)S(1)}, u32[]{:S(2)}, u32[]{:S(2)}) collective-permute-start(f32[216,128]{1,0:T(8,128)S(1)} %add.36), channel_id=1, source_target_pairs={{0,8},{2,10},{4,12},{6,14},{8,0},{10,2},{12,4},{14,6},{1,9},{3,11}... | collective-permute-start | bytes 331784 | tf_op jit(solution)/shard_map/ppermute | solution.py:416
  20.7 0.9 %dynamic-slice_bitcast_fusion.1.samp_ref = f32[16,1280]{1,0:T(8,128)S(1)} fusion(f32[8,16,1280]{2,1,0:T(8,128)} %constant.29.clone, s32[]{:T(128)S(6)} %select_n.23), kind=kLoop, calls=%fused_computation.3 | loop fusion | bytes 163844 | tf_op jit(solution)/shard_map/squeeze | solution.py:477
  21.6 1.9 %collective-permute-done.4 = f32[216,128]{1,0:T(8,128)S(1)} collective-permute-done((f32[216,128]{1,0:T(8,128)S(1)}, f32[216,128]{1,0:T(8,128)S(1)}, u32[]{:S(2)}, u32[]{:S(2)}) %collective-permute-start.4) | collective-permute-done | bytes 110624 | tf_op jit(solution)/shard_map/ppermute | solution.py:416
  23.6 3.0 %collective-permute-start.5 = (f32[216,128]{1,0:T(8,128)S(1)}, f32[216,128]{1,0:T(8,128)S(1)}, u32[]{:S(2)}, u32[]{:S(2)}) collective-permute-start(f32[216,128]{1,0:T(8,128)S(1)} %add.37), channel_id=1, source_target_pairs={{0,2},{2,0},{4,6},{6,4},{8,10},{10,8},{12,14},{14,12},{1,3},{3,1},... | collective-permute-start | bytes 331784 | tf_op jit(solution)/shard_map/ppermute | solution.py:416
  26.6 0.7 %dynamic-slice_bitcast_fusion.2.offset_ref = f32[8,512]{1,0:T(8,128)S(1)} fusion(f32[8,2,8,512]{3,2,1,0:T(8,128)} %constant.30.clone, s32[]{:T(128)S(6)} %select_n.23, s32[]{:T(128)S(6)} %select_n.22), kind=kLoop, calls=%fused_computation.4 | loop fusion | bytes 32776 | tf_op jit(solution)/shard_map/squeeze | solution.py:498
  27.3 2.0 %collective-permute-done.5 = f32[216,128]{1,0:T(8,128)S(1)} collective-permute-done((f32[216,128]{1,0:T(8,128)S(1)}, f32[216,128]{1,0:T(8,128)S(1)}, u32[]{:S(2)}, u32[]{:S(2)}) %collective-permute-start.5) | collective-permute-done | bytes 110624 | tf_op jit(solution)/shard_map/ppermute | solution.py:416
  29.3 0.1 collective-permute-start.6
  29.4 0.0 collective-permute-done.other_ref
  29.4 8.6 %shard_map.85 = (f32[432,512]{1,0:T(8,128)S(1)}, f32[432,256]{1,0:T(8,128)S(1)}, f32[432,256]{1,0:T(8,128)S(1)}, f32[432,128]{1,0:T(8,128)S(1)}, f32[432,128]{1,0:T(8,128)S(1)}) custom-call(f32[1728,128]{1,0:T(8,128)S(1)} %bitcast.15, f32[1728,128]{1,0:T(8,128)S(1)} %collective-permute-done.other_ref, f32[432,128]{1,0:T(8,128)S(1)} %get-tuple-element.18.mean_ref, ...), custom_call_target="tpu_custom_call" | custom-call | flops 6794772480 | bytes 2400256 | tf_op jit(solution)/shard_map/pallas_call | solution.py:431
  38.0 1.3 %collective-permute-start.7 = (f32[432,256]{1,0:T(8,128)S(1)}, f32[432,256]{1,0:T(8,128)S(1)}, u32[]{:S(2)}, u32[]{:S(2)}) collective-permute-start(f32[432,256]{1,0:T(8,128)S(1)} %get-tuple-element.24), channel_id=1, source_target_pairs={{2,0},{4,2},{6,4},{8,6},{10,8},{12,10},{14,12},{3,1},{5,3},{7,5},{... | collective-permute-start | bytes 1327112 | tf_op jit(solution)/shard_map/ppermute | solution.py:421
  39.3 4.6 %collective-permute-start.8 = (f32[432,256]{1,0:T(8,128)S(1)}, f32[432,256]{1,0:T(8,128)S(1)}, u32[]{:S(2)}, u32[]{:S(2)}) collective-permute-start(f32[432,256]{1,0:T(8,128)S(1)} %get-tuple-element.25), channel_id=1, source_target_pairs={{0,2},{2,4},{4,6},{6,8},{8,10},{10,12},{12,14},{1,3},{3,5},{5,7},{... | collective-permute-start | bytes 1327112 | tf_op jit(solution)/shard_map/ppermute | solution.py:421
  43.9 1.3 %collective-permute-start.9 = (f32[432,128]{1,0:T(8,128)S(1)}, f32[432,128]{1,0:T(8,128)S(1)}, u32[]{:S(2)}, u32[]{:S(2)}) collective-permute-start(f32[432,128]{1,0:T(8,128)S(1)} %get-tuple-element.26), channel_id=1, source_target_pairs={{4,0},{6,2},{8,4},{10,6},{12,8},{14,10},{5,1},{7,3},{9,5},{11,7},{... | collective-permute-start | bytes 663560 | tf_op jit(solution)/shard_map/ppermute | solution.py:421
  45.2 0.0 copy-start.2
  45.2 4.9 %collective-permute-start.10 = (f32[432,128]{1,0:T(8,128)S(1)}, f32[432,128]{1,0:T(8,128)S(1)}, u32[]{:S(2)}, u32[]{:S(2)}) collective-permute-start(f32[432,128]{1,0:T(8,128)S(1)} %get-tuple-element.27), channel_id=1, source_target_pairs={{0,4},{2,6},{4,8},{6,10},{8,12},{10,14},{1,5},{3,7},{5,9},{7,11},{... | collective-permute-start | bytes 663560 | tf_op jit(solution)/shard_map/ppermute | solution.py:421
  50.1 0.0 collective-permute-done.6.theirs_ref
  50.1 12.5 %shard_map.86 = (f32[432,432]{1,0:T(8,128)S(1)}, f32[16,512]{1,0:T(8,128)S(1)}) custom-call(s32[2]{0:T(128)S(1)} %pad_add_fusion.where_ref, f32[432,128]{1,0:T(8,128)S(1)} %maximum_select_fusion.mine_ref, f32[432,128]{1,0:T(8,128)S(1)} %collective-permute-done.6.theirs_ref), custom_call_target="tpu_custom_call" | custom-call | flops 20000000000 | bytes 442376 | tf_op jit(solution)/shard_map/pallas_call | solution.py:431
  62.6 0.0 collective-permute-done.9.rest_2_
  62.6 0.0 collective-permute-done.10.rest_3_
  62.6 0.0 collective-permute-done.7.rest_0_
  62.7 0.0 collective-permute-done.8.rest_1_
  62.7 7.0 %shard_map.87 = (f32[1296,128]{1,0:T(8,128)}, f32[324,128]{1,0:T(8,128)}, f32[81,128]{1,0:T(8,128)}, f32[27,128]{1,0:T(8,128)}) custom-call(s32[2]{0:T(128)S(1)} %pad_add_fusion.where_ref, f32[432,512]{1,0:T(8,128)S(1)} %get-tuple-element.19.own_ref, f32[432,128]{1,0:T(8,128)S(1)} %get-tuple-element.18.mean_ref, f32[16,512]{1,0:T(8,128)S(1)} %get-tuple-element.22.dev_ref, ...), custom_call_target="tpu_custom_call" | custom-call | flops 1146617856 | bytes 3621896 | tf_op jit(solution)/shard_map/pallas_call | solution.py:431
  (12 shorter events, 0.1 us)
Async XLA Ops:
  0.7 1.2 %copy-start = (f32[221184]{0:T(1024)S(1)}, f32[221184]{0:T(1024)}, u32[]{:S(2)}) copy-start(f32[221184]{0:T(1024)} %param.5) | copy-start | bytes 2654212
  1.9 13.0 %copy-start.3 = (f32[2,64,1280]{2,1,0:T(8,128)S(1)}, f32[2,64,1280]{2,1,0:T(8,128)}, u32[]{:S(2)}) copy-start(f32[2,64,1280]{2,1,0:T(8,128)} %constant.28.clone) | copy-start | bytes 1966084
  5.0 4.6 %copy-start.1 = (f32[221184]{0:T(1024)S(1)}, f32[221184]{0:T(1024)}, u32[]{:S(2)}) copy-start(f32[221184]{0:T(1024)} %param.5) | copy-start | bytes 2654212
  5.0 1.6 %collective-permute-start.1 = (f32[432,128]{1,0:T(8,128)S(1)}, f32[432,128]{1,0:T(8,128)S(1)}, u32[]{:S(2)}, u32[]{:S(2)}) collective-permute-start(f32[432,128]{1,0:T(8,128)S(1)} %get-tuple-element.21), channel_id=1, source_target_pairs={{0,1},{1,0},{2,3},{3,2},{4,5},{5,4},{6,7},{7,6},{8,9},{9,8},{10,11... | collective-permute-start | bytes 663560 | tf_op jit(solution)/shard_map/ppermute | solution.py:416
  6.7 6.3 %collective-permute-start.2 = (f32[216,128]{1,0:T(8,128)S(1)}, f32[216,128]{1,0:T(8,128)S(1)}, u32[]{:S(2)}, u32[]{:S(2)}) collective-permute-start(f32[216,128]{1,0:T(8,128)S(1)} %constant_dynamic-slice_fusion), channel_id=1, source_target_pairs={{0,2},{2,0},{4,6},{6,4},{8,10},{10,8},{12,14},{14,12},{1,3},{3,1},... | collective-permute-start | bytes 331784 | tf_op jit(solution)/shard_map/ppermute | solution.py:416
  9.7 19.8 %collective-permute-start = (f32[1728,128]{1,0:T(8,128)S(1)}, f32[1728,128]{1,0:T(8,128)S(1)}, u32[]{:S(2)}, u32[]{:S(2)}) collective-permute-start(f32[1728,128]{1,0:T(8,128)S(1)} %bitcast.14), channel_id=1, source_target_pairs={{0,1},{1,0},{2,3},{3,2},{4,5},{5,4},{6,7},{7,6},{8,9},{9,8},{10,11... | collective-permute-start | bytes 2654216 | tf_op jit(solution)/shard_map/ppermute | solution.py:416
  13.0 4.8 %collective-permute-start.3 = (f32[216,128]{1,0:T(8,128)S(1)}, f32[216,128]{1,0:T(8,128)S(1)}, u32[]{:S(2)}, u32[]{:S(2)}) collective-permute-start(f32[216,128]{1,0:T(8,128)S(1)} %dynamic-slice_add_fusion), channel_id=1, source_target_pairs={{0,4},{2,6},{4,0},{6,2},{8,12},{10,14},{12,8},{14,10},{1,5},{3,7},... | collective-permute-start | bytes 331784 | tf_op jit(solution)/shard_map/ppermute | solution.py:416
  17.9 5.7 %collective-permute-start.4 = (f32[216,128]{1,0:T(8,128)S(1)}, f32[216,128]{1,0:T(8,128)S(1)}, u32[]{:S(2)}, u32[]{:S(2)}) collective-permute-start(f32[216,128]{1,0:T(8,128)S(1)} %add.36), channel_id=1, source_target_pairs={{0,8},{2,10},{4,12},{6,14},{8,0},{10,2},{12,4},{14,6},{1,9},{3,11}... | collective-permute-start | bytes 331784 | tf_op jit(solution)/shard_map/ppermute | solution.py:416
  23.6 5.7 %collective-permute-start.5 = (f32[216,128]{1,0:T(8,128)S(1)}, f32[216,128]{1,0:T(8,128)S(1)}, u32[]{:S(2)}, u32[]{:S(2)}) collective-permute-start(f32[216,128]{1,0:T(8,128)S(1)} %add.37), channel_id=1, source_target_pairs={{0,2},{2,0},{4,6},{6,4},{8,10},{10,8},{12,14},{14,12},{1,3},{3,1},... | collective-permute-start | bytes 331784 | tf_op jit(solution)/shard_map/ppermute | solution.py:416
  29.3 20.8 %collective-permute-start.6 = (f32[432,128]{1,0:T(8,128)S(1)}, f32[432,128]{1,0:T(8,128)S(1)}, u32[]{:S(2)}, u32[]{:S(2)}) collective-permute-start(f32[432,128]{1,0:T(8,128)S(1)} %maximum_select_fusion.mine_ref), channel_id=1, source_target_pairs={{0,1},{1,0},{2,3},{3,2},{4,5},{5,4},{6,7},{7,6},{8,9},{9,8},{10,11... | collective-permute-start | bytes 663560 | tf_op jit(solution)/shard_map/ppermute | solution.py:416
  38.0 24.6 %collective-permute-start.7 = (f32[432,256]{1,0:T(8,128)S(1)}, f32[432,256]{1,0:T(8,128)S(1)}, u32[]{:S(2)}, u32[]{:S(2)}) collective-permute-start(f32[432,256]{1,0:T(8,128)S(1)} %get-tuple-element.24), channel_id=1, source_target_pairs={{2,0},{4,2},{6,4},{8,6},{10,8},{12,10},{14,12},{3,1},{5,3},{7,5},{... | collective-permute-start | bytes 1327112 | tf_op jit(solution)/shard_map/ppermute | solution.py:421
  39.3 23.3 %collective-permute-start.8 = (f32[432,256]{1,0:T(8,128)S(1)}, f32[432,256]{1,0:T(8,128)S(1)}, u32[]{:S(2)}, u32[]{:S(2)}) collective-permute-start(f32[432,256]{1,0:T(8,128)S(1)} %get-tuple-element.25), channel_id=1, source_target_pairs={{0,2},{2,4},{4,6},{6,8},{8,10},{10,12},{12,14},{1,3},{3,5},{5,7},{... | collective-permute-start | bytes 1327112 | tf_op jit(solution)/shard_map/ppermute | solution.py:421
  43.9 18.7 %collective-permute-start.9 = (f32[432,128]{1,0:T(8,128)S(1)}, f32[432,128]{1,0:T(8,128)S(1)}, u32[]{:S(2)}, u32[]{:S(2)}) collective-permute-start(f32[432,128]{1,0:T(8,128)S(1)} %get-tuple-element.26), channel_id=1, source_target_pairs={{4,0},{6,2},{8,4},{10,6},{12,8},{14,10},{5,1},{7,3},{9,5},{11,7},{... | collective-permute-start | bytes 663560 | tf_op jit(solution)/shard_map/ppermute | solution.py:421
  45.2 17.5 %copy-start.2 = (s32[768,128]{1,0:T(8,128)S(1)}, s32[768,128]{1,0:T(8,128)}, u32[]{:S(2)}) copy-start(s32[768,128]{1,0:T(8,128)} %constant.31.clone.chosen_ref) | copy-start | bytes 1179652
  45.2 17.4 %collective-permute-start.10 = (f32[432,128]{1,0:T(8,128)S(1)}, f32[432,128]{1,0:T(8,128)S(1)}, u32[]{:S(2)}, u32[]{:S(2)}) collective-permute-start(f32[432,128]{1,0:T(8,128)S(1)} %get-tuple-element.27), channel_id=1, source_target_pairs={{0,4},{2,6},{4,8},{6,10},{8,12},{10,14},{1,5},{3,7},{5,9},{7,11},{... | collective-permute-start | bytes 663560 | tf_op jit(solution)/shard_map/ppermute | solution.py:421

commit v2 on v1

v2 whole, which is shorter than its diff:
```python
import functools

import numpy as np
import jax
import jax.numpy as jnp
from jax import lax
from jax.experimental import pallas as pl
from jax.experimental.pallas import tpu as pltpu
from jax.sharding import PartitionSpec as P

BANDS = 432
LD = 32
SD = 16
LANES = 128
BLOCK = 128

alpha_lift = -1.586134342059924
beta_lift = -0.052980118572961
gamma_lift = 0.882911075530934
delta_lift = 0.443506852043971
scale_lift = 1.230174104914001


def split3(value):
    high = value.astype(jnp.bfloat16)
    rest = value - high.astype(jnp.float32)
    middle = rest.astype(jnp.bfloat16)
    return high, middle, (rest - middle.astype(jnp.float32)).astype(jnp.bfloat16)


def left_terms(parts, dim):
    high, middle, low = parts
    return jnp.concatenate([high, high, middle, high, low, middle], dim)


def right_terms(parts, dim):
    high, middle, low = parts
    return jnp.concatenate([high, middle, high, low, high, middle], dim)


def product_parts(left, right, left_dim, right_dim):
    return lax.dot_general(
        left_terms(left, left_dim),
        right_terms(right, right_dim),
        (((left_dim,), (right_dim,)), ((), ())),
        preferred_element_type=jnp.float32,
    )


def product(left, right, left_dim, right_dim):
    return product_parts(split3(left), split3(right), left_dim, right_dim)


def lift_rows(values):
    evens, odds = values[0::2], values[1::2]
    for weight_odd, weight_even in ((alpha_lift, beta_lift), (gamma_lift, delta_lift)):
        following = np.concatenate([evens[1:], evens[-1:]])
        odds = odds + weight_odd * (evens + following)
        preceding = np.concatenate([odds[:1], odds[:-1]])
        evens = evens + weight_even * (preceding + odds)
    return evens / scale_lift, odds * scale_lift


def axis_operators(length):
    operators = {}
    current = np.eye(length)
    for level in (1, 2, 3):
        low, high = lift_rows(current)
        operators[level, 0], operators[level, 1] = low, high
        current = low
    return operators


def output_lanes():
    lanes = []
    for level in (1, 2, 3):
        parts = [(1, 0), (0, 1), (1, 1)] + ([(0, 0)] if level == 3 else [])
        for line_part, samp_part in parts:
            for line in range(LD >> level):
                for samp in range(SD >> level):
                    lanes.append((level, line_part, samp_part, line, samp))
    return lanes


GROUP = LANES // SD
TILE_GROUPS = LD // GROUP
SHALLOW = (TILE_GROUPS + 1) * LANES
WIDE = SD // 2
LEVEL1 = 3 * (LD // 2) * WIDE
COUNT = LD * SD
FAR = COUNT // 16


def strip_lines(q):
    own = list(range(q * LD, (q + 1) * LD))
    groups = [list(range((1 - q) * LD + g * GROUP, (1 - q) * LD + (g + 1) * GROUP)) for g in range(TILE_GROUPS)]
    if q == 1:
        groups = groups[::-1]
    return own + [line for group in groups for line in group]


def neighbour_steps(p):
    near, far = 1 - 2 * (p & 1), 2 - 2 * (p & 2)
    return near, -near, far, -far


def build_constants(n_samp, n_line):
    lanes = output_lanes()
    line_ops = axis_operators(LD * n_line)
    samp_ops = axis_operators(SD * n_samp)
    line_own = np.zeros((n_line, n_line * LD, COUNT))
    for q in range(n_line):
        order = strip_lines(q)
        for o, (level, part, _, line, _) in enumerate(lanes):
            line_own[q, :, o] = line_ops[level, part][q * (LD >> level) + line][order]
    assert not line_own[:, SHALLOW // SD :, :LEVEL1].any()

    def reach(p, step):
        table = np.zeros((SD, COUNT))
        if 0 <= p + step < n_samp:
            for o, (level, _, part, _, samp) in enumerate(lanes):
                row = samp_ops[level, part][(p + step) * (SD >> level) + samp]
                table[:, o] = row[p * SD : (p + 1) * SD]
        return table

    size = COUNT + 5 * LANES
    line_table = np.zeros((n_line, n_line * LD, size))
    samp_table = np.zeros((n_samp, SD, size))
    line_table[:, :, :COUNT] = line_own
    for k in range(2):
        at = COUNT + k * LANES
        for line in range(LD // 2):
            for sb in range(3):
                for j in range(2):
                    source = (sb * (LD // 2) + line) * WIDE
                    line_table[:, :, at + line * WIDE + 2 * sb + j] = line_own[:, :, source]
        at = COUNT + (2 + k) * LANES
        line_table[:, :, at : at + LANES] = line_own[:, :, LEVEL1:]
        at = COUNT + 4 * LANES + k * FAR
        line_table[:, :, at : at + FAR] = line_own[:, :, COUNT - FAR :]
    offsets = np.zeros((n_samp, n_line, 8, COUNT))
    line_sums = line_own.sum(1)
    for p in range(n_samp):
        samp_table[p, :, :COUNT] = reach(p, 0)
        whole = reach(p, 0).sum(0)
        for k, step in enumerate(neighbour_steps(p)):
            given = reach(p, step)
            if k < 2:
                base = 0 if step > 0 else WIDE - 2
                left = given.copy()
                for line in range(LD // 2):
                    for sb in range(3):
                        for j in range(2):
                            source = (sb * (LD // 2) + line) * WIDE + base + j
                            samp_table[p, :, COUNT + k * LANES + line * WIDE + 2 * sb + j] = given[:, source]
                            left[:, source] = 0.0
                assert not left[:, :LEVEL1].any()
                at = COUNT + (2 + k) * LANES
                samp_table[p, :, at : at + LANES] = given[:, LEVEL1:]
            else:
                assert not given[:, : COUNT - FAR].any()
                at = COUNT + 4 * LANES + (k - 2) * FAR
                samp_table[p, :, at : at + FAR] = given[:, COUNT - FAR :]
            if 0 <= p + step < n_samp:
                sums = reach(p + step, -step).sum(0)
                offsets[p, :, k] = sums * line_sums
                whole = whole + sums
        offsets[p, :, 4] = whole * line_sums
        offsets[p, :, 4] -= offsets[p, :, :4].sum(1)
    return line_table.astype(np.float32), samp_table.astype(np.float32), offsets.astype(np.float32)


EDGES = list(range(0, BANDS, BLOCK)) + [BANDS]
LAST = EDGES[-1] - EDGES[-2]
OFF_DIAGONAL = ((1, 0), (2, 0), (2, 1), (3, 0), (3, 1), (3, 2))


def payload_rows(tiles):
    places = {}
    row = 2 * BLOCK
    for i, j in OFF_DIAGONAL:
        places[i, j] = row
        row += EDGES[i + 1] - EDGES[i]
    places["diagonal"] = row
    row += 8
    places["means"] = row
    row += 4 * tiles
    return places, -(-row // 32) * 32


def square_iotas():
    rows = lax.broadcasted_iota(jnp.int32, (BLOCK, BLOCK), 0)
    cols = lax.broadcasted_iota(jnp.int32, (BLOCK, BLOCK), 1)
    return rows, cols


def gram_kernel(tiles, where_ref, x_ref, send_ref, keep_ref, mean_ref, xs, pack):
    places, total = payload_rows(tiles)
    half = total // 2
    tile, line = where_ref[0], where_ref[1]
    parts = [x_ref[pl.ds(c, BANDS, stride=TILE_GROUPS), :] for c in range(TILE_GROUPS)]
    mean = jnp.sum(sum(parts[1:], parts[0]), axis=1, keepdims=True) / COUNT
    mean_ref[...] = jnp.broadcast_to(mean, (BANDS, LANES))
    for c in range(TILE_GROUPS):
        for k, part in enumerate(split3(parts[c] - mean)):
            xs[k, 0:BANDS, c * LANES : (c + 1) * LANES] = part
    xs[:, BANDS:, :] = jnp.zeros_like(xs[:, BANDS:, :])
    rows, cols = square_iotas()

    def rows_of(i):
        return [xs[k, 2 * i * BLOCK : 2 * (i + 1) * BLOCK, :] for k in range(3)]

    blocks = {}
    for i, j in ((0, 0), (1, 0), (1, 1)):
        square = product_parts(rows_of(i), rows_of(j), 1, 1)
        for a in range(2):
            for b in range(2):
                blocks[2 * i + a, 2 * j + b] = square[
                    a * BLOCK : (a + 1) * BLOCK, b * BLOCK : (b + 1) * BLOCK
                ]
    pack[places["diagonal"] :, :] = jnp.zeros_like(pack[places["diagonal"] :, :])
    for k in range(2):
        lower, upper = blocks[2 * k, 2 * k], blocks[2 * k + 1, 2 * k + 1]
        pack[k * BLOCK : (k + 1) * BLOCK, :] = jnp.where(rows >= cols, lower, upper)
        pack[places["diagonal"] + k : places["diagonal"] + k + 1, :] = jnp.sum(
            jnp.where(rows == cols, upper, 0.0), axis=0, keepdims=True
        )
    for i, j in OFF_DIAGONAL:
        height = EDGES[i + 1] - EDGES[i]
        pack[places[i, j] : places[i, j] + height, :] = blocks[i, j][:height]
    lane = lax.broadcasted_iota(jnp.int32, (BANDS, LANES), 1)
    mean_row = sum(
        lax.dot_general(
            jnp.ones((16, LANES), jnp.bfloat16),
            part,
            (((1,), (1,)), ((), ())),
            preferred_element_type=jnp.float32,
        )
        for part in split3(jnp.where(lane == 0, mean, 0.0))
    )
    which = lax.broadcasted_iota(jnp.int32, (tiles, BLOCK), 0)
    for c in range(4):
        width = EDGES[c + 1] - EDGES[c]
        place = places["means"] + c * tiles
        pack[place : place + tiles, 0:width] = jnp.where(
            which[:, :width] == tile, mean_row[0:1, EDGES[c] : EDGES[c + 1]], 0.0
        )
    keep_ref[...] = pack[pl.ds(pl.multiple_of(line * half, 8), half), :]
    send_ref[...] = pack[pl.ds(pl.multiple_of((1 - line) * half, 8), half), :]


def load_strip(where_ref, x_ref, other_ref, mean_ref, xs):
    mean = mean_ref[...]
    line = where_ref[1]
    for g in range(2 * TILE_GROUPS):
        if g < TILE_GROUPS:
            block = x_ref[pl.ds(g, BANDS, stride=TILE_GROUPS), :]
        else:
            k = g - TILE_GROUPS
            at = k + line * (TILE_GROUPS - 1 - 2 * k)
            block = other_ref[pl.ds(at, BANDS, stride=TILE_GROUPS), :]
        for k, part in enumerate(split3(block - mean)):
            xs[k, :, g * LANES : (g + 1) * LANES] = part


def strip_product(line_ref, samp_ref, xs, matrix, start, width, depth):
    samp = samp_ref[:, start : start + width]
    for line in range(depth // SD):
        values = samp * line_ref[line : line + 1, start : start + width]
        for k, part in enumerate(split3(values)):
            matrix[k, line * SD : (line + 1) * SD, 0:width] = part
    return product_parts(
        [xs[k, :, 0:depth] for k in range(3)], [matrix[k, 0:depth, 0:width] for k in range(3)], 1, 0
    )


def repacked(small, first, width):
    together = LANES // width
    height = BANDS // together
    lane = lax.broadcasted_iota(jnp.int32, (height, LANES), 1)
    result = jnp.zeros((height, LANES), jnp.float32)
    for k in range(together):
        taken = small[pl.ds(k, height, stride=together), :]
        moved = pltpu.roll(taken, (k * width - first) % LANES, 1)
        result = jnp.where((lane >= k * width) & (lane < (k + 1) * width), moved, result)
    return result


FAR_ROWS = BANDS * FAR // LANES
FAR_HELD = -(-FAR_ROWS // 8) * 8


def contribution_kernel(
    where_ref, x_ref, other_ref, mean_ref, line_ref, samp_ref, near1, near2, far1, far2, xs, matrix, small
):
    load_strip(where_ref, x_ref, other_ref, mean_ref, xs)
    run = functools.partial(strip_product, line_ref, samp_ref, xs, matrix)
    small[...] = run(COUNT + 4 * LANES, LANES, 2 * COUNT)
    for k, ref in enumerate((far1, far2)):
        ref[FAR_ROWS:, :] = jnp.zeros_like(ref[FAR_ROWS:, :])
        ref[0:FAR_ROWS, :] = repacked(small, k * FAR, FAR)
    first = run(COUNT, 2 * LANES, SHALLOW)
    near1[:, 0:LANES] = first[:, 0:LANES]
    near2[:, 0:LANES] = first[:, LANES:]
    second = run(COUNT + 2 * LANES, 2 * LANES, 2 * COUNT)
    near1[:, LANES:] = second[:, 0:LANES]
    near2[:, LANES:] = second[:, LANES:]


def own_kernel(where_ref, x_ref, other_ref, mean_ref, line_ref, samp_ref, own_ref, xs, matrix):
    load_strip(where_ref, x_ref, other_ref, mean_ref, xs)
    run = functools.partial(strip_product, line_ref, samp_ref, xs, matrix)
    own_ref[:, 0:LEVEL1] = run(0, LEVEL1, SHALLOW)
    own_ref[:, LEVEL1:] = run(LEVEL1, COUNT - LEVEL1, 2 * COUNT)


def spread(value):
    return jnp.broadcast_to(value, (8, LANES))


def added(terms):
    terms = list(terms)
    while len(terms) > 1:
        terms = [sum(terms[k + 1 : k + 2], terms[k]) for k in range(0, len(terms), 2)]
    return terms[0]


NEAR = 2


def inverse_factor(groups, held):
    rows = list(groups)
    lane = lax.broadcasted_iota(jnp.int32, (8, LANES), 1)
    sub = lax.broadcasted_iota(jnp.int32, (8, LANES), 0)
    done = []

    def columns(group, base):
        return [spread(group[:, base + t : base + t + 1]) for t in range(8)]

    following = columns(rows[0], 0)
    for b in range(len(rows)):
        base, slot = 8 * b, b % 2
        current = rows[b]
        for t in range(8):
            held[slot, t] = following[t]
        s = [[spread(held[slot, t, u : u + 1, :]) if u >= t else None for t in range(8)] for u in range(8)]
        inside = (lane >= base) & (lane < base + 8)
        start = jnp.where(inside, jnp.where(lane == base + sub, 1.0, 0.0), current)
        y = [spread(start[t : t + 1, :]) for t in range(8)]
        near = list(range(b + 1, min(len(rows), b + 1 + NEAR)))
        far = list(range(b + 1 + NEAR, len(rows)))
        g = {i: columns(rows[i], base) for i in near}
        if near:
            raw = columns(rows[b + 1], base + 8)
        r = [None] * 8
        l = [[None] * 8 for _ in range(8)]
        for p in range(8):
            r[p] = pl.reciprocal(s[p][p], approx=True)
            for t in range(p + 1, 8):
                l[t][p] = s[t][p] * r[p]
            for t in range(p + 1, 8):
                for u in range(t, 8):
                    if u == t == p + 1:
                        s[u][t] = s[u][t] - (s[u][p] * s[t][p]) * r[p]
                    else:
                        s[u][t] = s[u][t] - s[u][p] * l[t][p]
                for i in near:
                    g[i][t] = g[i][t] - g[i][p] * l[t][p]
                y[t] = y[t] - l[t][p] * y[p]
        scaled = {i: [g[i][p] * r[p] for p in range(8)] for i in near}
        if near:
            for p in range(8):
                held[slot, 8 + p] = scaled[b + 1][p]
            following = [
                raw[t] - added(g[b + 1][p] * spread(held[slot, 8 + p, t : t + 1, :]) for p in range(8))
                for t in range(8)
            ]
        for i in near:
            rows[i] = jnp.where(inside, 0.0, rows[i]) - added(scaled[i][p] * y[p] for p in range(8))
        if far:
            z = [None] * 8
            for t in range(7, -1, -1):
                z[t] = r[t] * y[t]
                for u in range(t + 1, 8):
                    z[t] = z[t] - l[u][t] * z[u]
            for i in far:
                old = columns(rows[i], base)
                rows[i] = jnp.where(inside, 0.0, rows[i]) - added(old[t] * z[t] for t in range(8))
        q, d = y[0], s[0][0]
        for t in range(1, 8):
            q = jnp.where(sub == t, y[t], q)
            d = jnp.where(sub == t, s[t][t], d)
        done.append(jnp.where(lane < base + 8, q * lax.rsqrt(d), 0.0))
    return done


def whiten_kernel(tiles, where_ref, mine_ref, theirs_ref, w_ref, dev_ref, pack, a, held):
    places, total = payload_rows(tiles)
    half = total // 2
    line = where_ref[1]
    pack[pl.ds(pl.multiple_of(line * half, 8), half), :] = mine_ref[...]
    pack[pl.ds(pl.multiple_of((1 - line) * half, 8), half), :] = theirs_ref[...]
    at = places["means"]
    means = jnp.concatenate([pack[at + c * tiles : at + (c + 1) * tiles, :] for c in range(4)], 1)
    dev = means - jnp.sum(means, axis=0, keepdims=True) / tiles
    dev_ref[...] = dev
    between = (LD * SD) * product(dev, dev, 0, 0)
    rows, cols = square_iotas()
    trace = jnp.zeros((1, BLOCK), jnp.float32)
    for k in range(2):
        packed = pack[k * BLOCK : (k + 1) * BLOCK, :]
        turned = packed.T
        diagonal = pack[places["diagonal"] + k : places["diagonal"] + k + 1, :]
        lower = jnp.where(rows >= cols, packed, turned)
        upper = jnp.where(rows < cols, packed, jnp.where(rows > cols, turned, diagonal))
        for i, full in ((2 * k, lower), (2 * k + 1, upper)):
            low, high = EDGES[i], EDGES[i + 1]
            full = full + between[i * BLOCK : (i + 1) * BLOCK, i * BLOCK : (i + 1) * BLOCK]
            trace += jnp.sum(jnp.where(rows == cols, full, 0.0), axis=0, keepdims=True)
            a[low:high, i * BLOCK : (i + 1) * BLOCK] = full[: high - low]
    for i, j in OFF_DIAGONAL:
        low, high = EDGES[i], EDGES[i + 1]
        a[low:high, j * BLOCK : (j + 1) * BLOCK] = (
            pack[places[i, j] : places[i, j] + high - low, :]
            + between[low:high, j * BLOCK : (j + 1) * BLOCK]
        )
    load = 0.01 * (jnp.sum(trace, axis=1, keepdims=True) / BANDS)
    for i in range(4):
        low, high = EDGES[i], EDGES[i + 1]
        full = a[low:high, i * BLOCK : (i + 1) * BLOCK]
        height = high - low
        a[low:high, i * BLOCK : (i + 1) * BLOCK] = full + jnp.where(
            (rows == cols)[:height], load, 0.0
        )
    w_ref[...] = jnp.zeros_like(w_ref)
    for k in range(4):
        low, high = EDGES[k], EDGES[k + 1]
        groups = [a[low + 8 * g : low + 8 * g + 8, low : low + BLOCK] for g in range((high - low) // 8)]
        m = jnp.concatenate(inverse_factor(groups, held), 0)[:, : high - low]
        if k:
            w_ref[low:high, :low] = product(m, w_ref[low:high, :low], 1, 0)
        w_ref[low:high, low:high] = m
        if high < BANDS:
            parts = split3(m)
            factor = split3(product_parts(split3(a[high:, low:high]), parts, 1, 1))
            a[high:, high:BANDS] = a[high:, high:BANDS] - product_parts(factor, factor, 1, 1)
            w_ref[high:, :high] = w_ref[high:, :high] - product_parts(factor, split3(w_ref[low:high, :high]), 1, 0)


def output_kernel(
    n_line, pixels, where_ref, own_ref, dev_ref, w_ref, offset_ref, near1, near2, far_ref, *rest
):
    (out1_ref, out2_ref, out3_ref, approx_ref), (d, small) = rest[:4], rest[4:]
    tile, samp = where_ref[0], where_ref[2]
    bit = samp % 2
    tiles = dev_ref.shape[0]
    which = lax.broadcasted_iota(jnp.int32, (tiles, COUNT), 0)
    near, far = 1 - 2 * bit, 2 - 4 * ((samp // 2) % 2)
    gains = jnp.where(which == tile, offset_ref[4:5, :], 0.0)
    for k, step in enumerate((near, -near, far, -far)):
        gains += jnp.where(which == tile + n_line * step, offset_ref[k : k + 1, :], 0.0)
    shift = product(dev_ref[:, 0:BANDS], gains, 0, 0)
    together = LANES // FAR
    lane = lax.broadcasted_iota(jnp.int32, (FAR_ROWS, LANES), 1)
    for k in range(together):
        moved = pltpu.roll(far_ref[0:FAR_ROWS, :], LANES - FAR - k * FAR, 1)
        small[pl.ds(k, FAR_ROWS, stride=together), :] = jnp.where(lane >= LANES - FAR, moved, 0.0)
    lane = lax.broadcasted_iota(jnp.int32, (BANDS, LANES), 1) % WIDE
    scale = float(pixels) ** 0.5

    def keep(at, value):
        for k, part in enumerate(split3(value * scale)):
            d[k, :, at : at + LANES] = part

    bases = ((WIDE - 2) * (1 - bit), (WIDE - 2) * bit)
    for sb in range(3):
        at = sb * LANES
        value = own_ref[:, at : at + LANES] + shift[:, at : at + LANES]
        for base, ref in zip(bases, (near1, near2)):
            moved = pltpu.roll(ref[:, 0:LANES], (base - 2 * sb + LANES) % LANES, 1)
            value += jnp.where((lane >= base) & (lane < base + 2), moved, 0.0)
        keep(at, value)
    keep(
        LEVEL1,
        own_ref[:, LEVEL1:] + shift[:, LEVEL1:] + near1[:, LANES:] + near2[:, LANES:] + small[...],
    )
    for low, high in ((0, 2 * BLOCK), (2 * BLOCK, BANDS)):
        w = split3(w_ref[low:high, :high])
        out = product_parts(w, [d[k, 0:high, :] for k in range(3)], 1, 0)
        for sb in range(3):
            out1_ref[sb * BANDS + low : sb * BANDS + high, :] = out[:, sb * LANES : (sb + 1) * LANES]
        small[low:high, :] = out[:, LEVEL1:]
    size2, size3 = COUNT // 16, COUNT // 64
    rows2, rows3 = BANDS * size2 // LANES, BANDS * size3 // LANES
    for sb in range(3):
        out2_ref[sb * rows2 : (sb + 1) * rows2, :] = repacked(small, sb * size2, size2)
        out3_ref[sb * rows3 : (sb + 1) * rows3, :] = repacked(small, 3 * size2 + sb * size3, size3)
    approx_ref[...] = repacked(small, 3 * size2 + 3 * size3, size3)


def permuted(array, axis, partner):
    count = lax.axis_size(axis)
    return lax.ppermute(array, axis, [(i, partner(i)) for i in range(count) if 0 <= partner(i) < count])


def mirrored(size):
    def partner(i):
        within = i % size
        return i - within + 2 * (size // 2 - 1 - within // 2) + within % 2

    return partner


VMEM = pl.BlockSpec(memory_space=pltpu.VMEM)
SMEM = pl.BlockSpec(memory_space=pltpu.SMEM)


def call(kernel, name, shapes, inputs, scratch, flops):
    specs = [SMEM if value.dtype == jnp.int32 and value.ndim == 1 else VMEM for value in inputs]
    size = sum(value.size * 4 for value in inputs)
    return pl.pallas_call(
        kernel,
        name=name,
        out_shape=[jax.ShapeDtypeStruct(shape, jnp.float32) for shape in shapes],
        in_specs=specs,
        out_specs=[VMEM] * len(shapes),
        scratch_shapes=[pltpu.VMEM(shape, dtype) for shape, dtype in scratch],
        compiler_params=pltpu.CompilerParams(vmem_limit_bytes=40 * 2**20),
        cost_estimate=pl.CostEstimate(flops=flops, bytes_accessed=size, transcendentals=0),
    )(*inputs)


def local(constants, cube):
    line_table, samp_table, offset_table = (jnp.asarray(table) for table in constants)
    n_samp, n_line = lax.axis_size("samp"), lax.axis_size("line")
    tiles = n_samp * n_line
    samp, line = lax.axis_index("samp"), lax.axis_index("line")
    where = jnp.stack([samp * n_line + line, line, samp]).astype(jnp.int32)
    f32, bf16 = jnp.float32, jnp.bfloat16
    x = cube.reshape(BANDS * COUNT // LANES, LANES)
    other = permuted(x, "line", lambda i: i ^ 1)
    _, total = payload_rows(tiles)
    half, quarter = total // 2, total // 4
    send, keep, mean = call(
        functools.partial(gram_kernel, tiles),
        "gram",
        [(half, LANES), (half, LANES), (BANDS, LANES)],
        [where, x],
        [((3, 4 * BLOCK, COUNT), bf16), ((total, LANES), f32)],
        2 * BANDS * BANDS * COUNT * 4,
    )
    summed = keep + permuted(send, "line", lambda i: i ^ 1)
    side = ((samp >> 1) ^ (samp >> 2)) & 1
    kept = lax.dynamic_slice_in_dim(summed, side * quarter, quarter, 0)
    given = lax.dynamic_slice_in_dim(summed, (1 - side) * quarter, quarter, 0)
    kept = kept + permuted(given, "samp", lambda i: i ^ 2)

    strip_scratch = [((3, BANDS, 2 * COUNT), bf16), ((3, 2 * COUNT, LEVEL1), bf16)]
    lines, samps = line_table[line], samp_table[samp]
    near1, near2, far1, far2 = call(
        contribution_kernel,
        "contributions",
        [(BANDS, 2 * LANES)] * 2 + [(FAR_HELD, LANES)] * 2,
        [where, x, other, mean, lines, samps],
        strip_scratch + [((BANDS, LANES), f32)],
        2 * BANDS * 2 * COUNT * 5 * LANES * 6,
    )
    kept, near1, near2 = lax.optimization_barrier((kept, near1, near2))
    kept2 = kept + permuted(kept, "samp", lambda i: i ^ 1)
    mean_later, _ = lax.optimization_barrier((mean, kept))
    (own,) = call(
        own_kernel,
        "own",
        [(BANDS, COUNT)],
        [where, x, other, mean_later, lines, samps],
        strip_scratch,
        2 * BANDS * 2 * COUNT * COUNT * 6,
    )
    kept, own = lax.optimization_barrier((kept2, own))
    far = jnp.zeros_like(far2)
    size = 8
    while size <= n_samp:
        partner = mirrored(size)
        both = permuted(jnp.concatenate([kept, far2]), "samp", partner)
        kept = kept + both[:quarter]
        adjacent = jnp.asarray([abs(partner(i) - i) == 2 for i in range(n_samp)])[samp]
        far = far + jnp.where(adjacent, both[quarter:], 0.0)
        size *= 2
    both = permuted(jnp.concatenate([kept, far1]), "samp", lambda i: i ^ 2)
    back = both[:quarter]
    far = far + both[quarter:]
    mine = jnp.where(side == 0, jnp.concatenate([kept, back]), jnp.concatenate([back, kept]))
    theirs = permuted(mine, "line", lambda i: i ^ 1)
    near1 = permuted(near1, "samp", lambda i: i ^ 1)
    near2 = permuted(near2, "samp", lambda i: ((i + 1) ^ 1) - 1)

    w, dev = call(
        functools.partial(whiten_kernel, tiles),
        "whiten",
        [(BANDS, BANDS), (tiles, 4 * BLOCK)],
        [where, mine, theirs],
        [((total, LANES), f32), ((BANDS, 4 * BLOCK), f32), ((2, 16, 8, LANES), f32)],
        2 * 10**10,
    )
    outs = call(
        functools.partial(output_kernel, n_line, COUNT * tiles),
        "outputs",
        [
            (3 * BANDS * (COUNT // 4) // LANES, LANES),
            (3 * BANDS * (COUNT // 16) // LANES, LANES),
            (3 * BANDS * (COUNT // 64) // LANES, LANES),
            (BANDS * (COUNT // 64) // LANES, LANES),
        ],
        [where, own, dev, w, offset_table[samp, line], near1, near2, far],
        [((3, BANDS, COUNT), bf16), ((BANDS, LANES), f32)],
        2 * BANDS * BANDS * COUNT * 6,
    )
    return tuple(out.reshape(-1) for out in outs)


def solution(mesh):
    n_samp, n_line = mesh.shape["samp"], mesh.shape["line"]
    assert n_line == 2 and n_samp >= 8 and n_samp & (n_samp - 1) == 0
    constants = build_constants(n_samp, n_line)
    spec = P(("groups", "samp", "line"))
    return jax.shard_map(
        functools.partial(local, constants),
        mesh=mesh,
        in_specs=(spec,),
        out_specs=(spec,) * 4,
        check_vma=False,
    )
```

time: 70 us -> 58.2 us (0.83)
  starting transfers between devices: 23.3 us -> 13.5 us
  Pallas kernels: 31.2 us -> 26.3 us
  local copies, waits for them, and re-layouts: 2.83 us -> 4.47 us
    ppermute x11 -> x9, starting transfers between devices: 23.3 us -> 13.5 us  [permuted(): lax.ppermute(array, axis, [(i, partner(i)) for i in range(count) if 0 <=...]
    pallas_call x4 -> x5, Pallas kernels: 31.2 us -> 26.3 us  [call(): pl.pallas_call(kernel, name=name, out_shape=[jax.ShapeDtypeStruct(shape,...]
    squeeze x3, local copies, waits for them, and re-layouts: 1.63 us -> 2.67 us  [the longest x2 1.95 us: local(): lines, samps = (line_table[line], samp_table[samp])]
    ppermute x11 -> x9, waiting for transfers between devices: 11.4 us -> 12 us  [permuted(): lax.ppermute(array, axis, [(i, partner(i)) for i in range(count) if 0 <=...]
  transfers between devices with their start and end apart: 11 -> 9, of which waited for: 5 -> 6; matrix products, arithmetic and copies ran while one was open for 2% -> 7% of each run, Pallas kernels for 30% -> 31%
where the time goes in v2:
time: 58.2 us; the launch traced here: 57.9 us
  Pallas kernels  26.3 us (45%)
  starting transfers between devices  13.5 us (23%)
  waiting for transfers between devices  12 us (21%)
  local copies, waits for them, and re-layouts  4.47 us (8%)
  other arithmetic  0.86 us (1%)
  between operations  0.79 us (1%)
    pallas_call x5, Pallas kernels, call(): pl.pallas_call(kernel, name=name, out_shape=[jax.ShapeDtypeStruct(shape,...  26.3 us
    ppermute x9, starting transfers between devices, permuted(): lax.ppermute(array, axis, [(i, partner(i)) for i in range(count) if 0 <=...  13.5 us
    ppermute x9, waiting for transfers between devices, permuted(): lax.ppermute(array, axis, [(i, partner(i)) for i in range(count) if 0 <=...  12 us
    squeeze x2, local copies, waits for them, and re-layouts, local(): lines, samps = (line_table[line], samp_table[samp])  1.95 us
    unnamed x10, local copies, waits for them, and re-layouts  1.19 us
  transfers between devices with their start and end apart: 9, of which 6 were waited for; matrix products, arithmetic and copies ran while one was open for 7% of the time, Pallas kernels for 31%

profile of v2, /device:TPU:0, one launch (start us, length us, event | category | flops | bytes accessed | tf_op | source)
XLA Modules:
  0.0 57.9 jit_solution(2213806094243153087)
XLA Ops:
  0.6 0.5 collective-permute-start.2
  1.1 0.1 pad_add_fusion.where_ref
  1.2 1.2 %copy-done = f32[221184]{0:T(1024)S(1)} copy-done((f32[221184]{0:T(1024)S(1)}, f32[221184]{0:T(1024)}, u32[]{:S(2)}) %copy-start) | copy-done | bytes 884760
  2.4 2.4 %gram.1 = (f32[432,128]{1,0:T(8,128)S(1)}, f32[432,128]{1,0:T(8,128)S(1)}, f32[432,128]{1,0:T(8,128)S(1)}) custom-call(s32[3]{0:T(128)S(1)} %pad_add_fusion.where_ref, f32[1728,128]{1,0:T(8,128)S(1)} %bitcast.16), custom_call_target="tpu_custom_call" | custom-call | flops 764411904 | bytes 884748 | tf_op jit(solution)/shard_map/gram/pallas_call | solution.py:521
  4.8 0.1 collective-permute-start
  4.9 1.1 %dynamic-slice_bitcast_fusion.line_ref = f32[64,1152]{1,0:T(8,128)S(1)} fusion(f32[2,64,1152]{2,1,0:T(8,128)} %constant.30.clone, s32[]{:T(128)S(6)} %select_n.33), kind=kLoop, calls=%fused_computation | loop fusion | bytes 589828 | tf_op jit(solution)/shard_map/squeeze | solution.py:559
  6.0 0.4 collective-permute-done
  6.4 2.8 %collective-permute-start.1 = (f32[216,128]{1,0:T(8,128)S(1)}, f32[216,128]{1,0:T(8,128)S(1)}, u32[]{:S(2)}, u32[]{:S(2)}) collective-permute-start(f32[216,128]{1,0:T(8,128)S(1)} %constant_dynamic-slice_fusion), channel_id=1, source_target_pairs={{0,4},{2,6},{4,0},{6,2},{8,12},{10,14},{12,8},{14,10},{1,5},{3,7},... | collective-permute-start | bytes 331784 | tf_op jit(solution)/shard_map/ppermute | solution.py:503
  9.2 0.9 %dynamic-slice_bitcast_fusion.1.samp_ref = f32[16,1152]{1,0:T(8,128)S(1)} fusion(f32[8,16,1152]{2,1,0:T(8,128)} %constant.31.clone, s32[]{:T(128)S(6)} %select_n.34), kind=kLoop, calls=%fused_computation.6 | loop fusion | bytes 147460 | tf_op jit(solution)/shard_map/squeeze | solution.py:559
  10.0 2.7 %collective-permute-done.1 = f32[216,128]{1,0:T(8,128)S(1)} collective-permute-done((f32[216,128]{1,0:T(8,128)S(1)}, f32[216,128]{1,0:T(8,128)S(1)}, u32[]{:S(2)}, u32[]{:S(2)}) %collective-permute-start.1) | collective-permute-done | bytes 110624 | tf_op jit(solution)/shard_map/ppermute | solution.py:503
  12.8 0.0 collective-permute-done.2.other_ref
  12.8 5.1 %contributions.1 = (f32[432,256]{1,0:T(8,128)S(1)}, f32[432,256]{1,0:T(8,128)S(1)}, f32[112,128]{1,0:T(8,128)S(1)}, f32[112,128]{1,0:T(8,128)S(1)}) custom-call(s32[3]{0:T(128)S(1)} %pad_add_fusion.where_ref, f32[1728,128]{1,0:T(8,128)S(1)} %bitcast.17, f32[1728,128]{1,0:T(8,128)S(1)} %collective-permute-done.2.other_ref, ...), custom_call_target="tpu_custom_call" | custom-call | flops 3397386240 | bytes 2359308 | tf_op jit(solution)/shard_map/contributions/pallas_call | solution.py:521
  17.9 1.7 %collective-permute-start.3 = (f32[216,128]{1,0:T(8,128)S(1)}, f32[216,128]{1,0:T(8,128)S(1)}, u32[]{:S(2)}, u32[]{:S(2)}) collective-permute-start(f32[216,128]{1,0:T(8,128)S(1)} %dynamic-slice_add_fusion), channel_id=1, source_target_pairs={{0,2},{2,0},{4,6},{6,4},{8,10},{10,8},{12,14},{14,12},{1,3},{3,1},... | collective-permute-start | bytes 331784 | tf_op jit(solution)/shard_map/ppermute | solution.py:503
  19.7 4.4 %own.1.own_ref = f32[432,512]{1,0:T(8,128)S(1)} custom-call(s32[3]{0:T(128)S(1)} %pad_add_fusion.where_ref, f32[1728,128]{1,0:T(8,128)S(1)} %bitcast.18, f32[1728,128]{1,0:T(8,128)S(1)} %collective-permute-done.2.other_ref, f32[432,128]{1,0:T(8,128)S(1)} %get-tuple-element.29.mean_ref, f32[64,1152]{1,0:T(8,128)S(1)} %dynamic-slice_bitcast_fusion.line_ref, ...), custom_call_target="tpu_custom_call" | custom-call | flops 2717908992 | bytes 2359308 | tf_op jit(solution)/shard_map/own/pallas_call | solution.py:521
  24.0 0.0 collective-permute-done.3
  24.1 3.7 %collective-permute-start.4 = (f32[328,128]{1,0:T(8,128)S(1)}, f32[328,128]{1,0:T(8,128)S(1)}, u32[]{:S(2)}, u32[]{:S(2)}) collective-permute-start(f32[328,128]{1,0:T(8,128)S(1)} %pad_maximum_fusion), channel_id=1, source_target_pairs={{0,12},{2,14},{4,8},{6,10},{8,4},{10,6},{12,0},{14,2},{1,13},{3,15... | collective-permute-start | bytes 503816 | tf_op jit(solution)/shard_map/ppermute | solution.py:503
  27.8 3.8 %collective-permute-done.4 = f32[328,128]{1,0:T(8,128)S(1)} collective-permute-done((f32[328,128]{1,0:T(8,128)S(1)}, f32[328,128]{1,0:T(8,128)S(1)}, u32[]{:S(2)}, u32[]{:S(2)}) %collective-permute-start.4) | collective-permute-done | bytes 167968 | tf_op jit(solution)/shard_map/ppermute | solution.py:503
  31.7 0.0 copy-start.4
  31.7 3.3 %collective-permute-start.5 = (f32[328,128]{1,0:T(8,128)S(1)}, f32[328,128]{1,0:T(8,128)S(1)}, u32[]{:S(2)}, u32[]{:S(2)}) collective-permute-start(f32[328,128]{1,0:T(8,128)S(1)} %pad_maximum_fusion.1), channel_id=1, source_target_pairs={{0,4},{2,6},{4,0},{6,2},{8,12},{10,14},{12,8},{14,10},{1,5},{3,7},... | collective-permute-start | bytes 503816 | tf_op jit(solution)/shard_map/ppermute | solution.py:503
  34.9 0.6 %dynamic_slice.23 = pred[1]{0:T(512)(128)(4,1)} dynamic-slice(pred[8]{0:T(512)(128)(4,1)S(1)} %copy-done.4, s32[]{:T(128)S(6)} %select_n.34), dynamic_slice_sizes={1} | dynamic-slice | bytes 6 | tf_op jit(solution)/shard_map/dynamic_slice | solution.py:586
  35.5 0.7 %dynamic-slice_bitcast_fusion.2.offset_ref = f32[8,512]{1,0:T(8,128)S(1)} fusion(f32[8,2,8,512]{3,2,1,0:T(8,128)} %constant.32.clone, s32[]{:T(128)S(6)} %select_n.34, s32[]{:T(128)S(6)} %select_n.33), kind=kLoop, calls=%fused_computation.9 | loop fusion | bytes 32776 | tf_op jit(solution)/shard_map/squeeze | solution.py:614
  36.2 0.5 collective-permute-start.7
  36.7 0.9 %collective-permute-start.8 = (f32[432,256]{1,0:T(8,128)S(1)}, f32[432,256]{1,0:T(8,128)S(1)}, u32[]{:S(2)}, u32[]{:S(2)}) collective-permute-start(f32[432,256]{1,0:T(8,128)S(1)} %get-tuple-element.37), channel_id=1, source_target_pairs={{2,4},{4,2},{6,8},{8,6},{10,12},{12,10},{3,5},{5,3},{7,9},{9,7},{1... | collective-permute-start | bytes 1327112 | tf_op jit(solution)/shard_map/ppermute | solution.py:503
  37.6 0.9 %collective-permute-done.5 = f32[328,128]{1,0:T(8,128)S(1)} collective-permute-done((f32[328,128]{1,0:T(8,128)S(1)}, f32[328,128]{1,0:T(8,128)S(1)}, u32[]{:S(2)}, u32[]{:S(2)}) %collective-permute-start.5) | collective-permute-done | bytes 167968 | tf_op jit(solution)/shard_map/ppermute | solution.py:503
  38.5 0.1 collective-permute-start.6
  38.6 0.7 %slice_add_fusion.1.far_ref = f32[112,128]{1,0:T(8,128)S(1)} fusion(f32[328,128]{1,0:T(8,128)S(1)} %collective-permute-done.5, f32[328,128]{1,0:T(8,128)S(1)} %collective-permute-done.4, pred[]{:T(512)} %bitcast.7), kind=kLoop, calls=%fused_computation.7 | loop fusion | flops 28672 | bytes 172033 | tf_op jit(solution)/shard_map/add | solution.py:591
  39.3 0.0 copy-start.3
  39.3 0.8 %collective-permute-done.6.theirs_ref = f32[432,128]{1,0:T(8,128)S(1)} collective-permute-done((f32[432,128]{1,0:T(8,128)S(1)}, f32[432,128]{1,0:T(8,128)S(1)}, u32[]{:S(2)}, u32[]{:S(2)}) %collective-permute-start.6) | collective-permute-done | bytes 221216 | tf_op jit(solution)/shard_map/ppermute | solution.py:503
  40.1 11.1 %whiten.1 = (f32[432,432]{1,0:T(8,128)S(1)}, f32[16,512]{1,0:T(8,128)S(1)}) custom-call(s32[3]{0:T(128)S(1)} %pad_add_fusion.where_ref, f32[432,128]{1,0:T(8,128)S(1)} %maximum_select_fusion.mine_ref, f32[432,128]{1,0:T(8,128)S(1)} %collective-permute-done.6.theirs_ref), custom_call_target="tpu_custom_call" | custom-call | flops 20000000000 | bytes 442380 | tf_op jit(solution)/shard_map/whiten/pallas_call | solution.py:521
  51.2 3.4 %collective-permute-done.7.near1 = f32[432,256]{1,0:T(8,128)S(1)} collective-permute-done((f32[432,256]{1,0:T(8,128)S(1)}, f32[432,256]{1,0:T(8,128)S(1)}, u32[]{:S(2)}, u32[]{:S(2)}) %collective-permute-start.7) | collective-permute-done | bytes 442400 | tf_op jit(solution)/shard_map/ppermute | solution.py:503
  54.6 0.0 collective-permute-done.8.near2
  54.6 3.3 %outputs.1 = (f32[1296,128]{1,0:T(8,128)}, f32[324,128]{1,0:T(8,128)}, f32[81,128]{1,0:T(8,128)}, f32[27,128]{1,0:T(8,128)}) custom-call(s32[3]{0:T(128)S(1)} %pad_add_fusion.where_ref, f32[432,512]{1,0:T(8,128)S(1)} %copy-done.3, f32[16,512]{1,0:T(8,128)S(1)} %get-tuple-element.34.dev_ref, f32[432,432]{1,0:T(8,128)S(1)} %get-tuple-element.35.w_ref, ...), custom_call_target="tpu_custom_call" | custom-call | flops 1146617856 | bytes 2622476 | tf_op jit(solution)/shard_map/outputs/pallas_call | solution.py:521
  (16 shorter events, 0.2 us)
Async XLA Ops:
  0.6 12.1 %collective-permute-start.2 = (f32[1728,128]{1,0:T(8,128)}, f32[1728,128]{1,0:T(8,128)S(1)}, u32[]{:S(2)}, u32[]{:S(2)}) collective-permute-start(f32[1728,128]{1,0:T(8,128)} %bitcast.15), channel_id=1, source_target_pairs={{0,1},{1,0},{2,3},{3,2},{4,5},{5,4},{6,7},{7,6},{8,9},{9,8},{10,11... | collective-permute-start | bytes 2654216 | tf_op jit(solution)/shard_map/ppermute | solution.py:503
  1.2 1.2 %copy-start = (f32[221184]{0:T(1024)S(1)}, f32[221184]{0:T(1024)}, u32[]{:S(2)}) copy-start(f32[221184]{0:T(1024)} %param.5) | copy-start | bytes 2654212
  4.8 1.5 %collective-permute-start = (f32[432,128]{1,0:T(8,128)S(1)}, f32[432,128]{1,0:T(8,128)S(1)}, u32[]{:S(2)}, u32[]{:S(2)}) collective-permute-start(f32[432,128]{1,0:T(8,128)S(1)} %get-tuple-element.24), channel_id=1, source_target_pairs={{0,1},{1,0},{2,3},{3,2},{4,5},{5,4},{6,7},{7,6},{8,9},{9,8},{10,11... | collective-permute-start | bytes 663560 | tf_op jit(solution)/shard_map/ppermute | solution.py:503
  4.9 7.9 %copy-start.1 = (f32[221184]{0:T(1024)S(1)}, f32[221184]{0:T(1024)}, u32[]{:S(2)}) copy-start(f32[221184]{0:T(1024)} %param.5) | copy-start | bytes 2654212
  6.4 6.4 %collective-permute-start.1 = (f32[216,128]{1,0:T(8,128)S(1)}, f32[216,128]{1,0:T(8,128)S(1)}, u32[]{:S(2)}, u32[]{:S(2)}) collective-permute-start(f32[216,128]{1,0:T(8,128)S(1)} %constant_dynamic-slice_fusion), channel_id=1, source_target_pairs={{0,4},{2,6},{4,0},{6,2},{8,12},{10,14},{12,8},{14,10},{1,5},{3,7},... | collective-permute-start | bytes 331784 | tf_op jit(solution)/shard_map/ppermute | solution.py:503
  17.9 6.1 %collective-permute-start.3 = (f32[216,128]{1,0:T(8,128)S(1)}, f32[216,128]{1,0:T(8,128)S(1)}, u32[]{:S(2)}, u32[]{:S(2)}) collective-permute-start(f32[216,128]{1,0:T(8,128)S(1)} %dynamic-slice_add_fusion), channel_id=1, source_target_pairs={{0,2},{2,0},{4,6},{6,4},{8,10},{10,8},{12,14},{14,12},{1,3},{3,1},... | collective-permute-start | bytes 331784 | tf_op jit(solution)/shard_map/ppermute | solution.py:503
  24.0 7.6 %copy-start.2 = (f32[432,512]{1,0:T(8,128)}, f32[432,512]{1,0:T(8,128)S(1)}, u32[]{:S(2)}) copy-start(f32[432,512]{1,0:T(8,128)S(1)} %own.1.own_ref) | copy-start | bytes 2654212
  24.1 7.5 %collective-permute-start.4 = (f32[328,128]{1,0:T(8,128)S(1)}, f32[328,128]{1,0:T(8,128)S(1)}, u32[]{:S(2)}, u32[]{:S(2)}) collective-permute-start(f32[328,128]{1,0:T(8,128)S(1)} %pad_maximum_fusion), channel_id=1, source_target_pairs={{0,12},{2,14},{4,8},{6,10},{8,4},{10,6},{12,0},{14,2},{1,13},{3,15... | collective-permute-start | bytes 503816 | tf_op jit(solution)/shard_map/ppermute | solution.py:503
  31.7 3.3 %copy-start.4 = (pred[8]{0:T(512)(128)(4,1)S(1)}, pred[8]{0:T(512)(128)(4,1)}, u32[]{:S(2)}) copy-start(pred[8]{0:T(512)(128)(4,1)} %constant.33.clone) | copy-start | bytes 28
  31.7 6.8 %collective-permute-start.5 = (f32[328,128]{1,0:T(8,128)S(1)}, f32[328,128]{1,0:T(8,128)S(1)}, u32[]{:S(2)}, u32[]{:S(2)}) collective-permute-start(f32[328,128]{1,0:T(8,128)S(1)} %pad_maximum_fusion.1), channel_id=1, source_target_pairs={{0,4},{2,6},{4,0},{6,2},{8,12},{10,14},{12,8},{14,10},{1,5},{3,7},... | collective-permute-start | bytes 503816 | tf_op jit(solution)/shard_map/ppermute | solution.py:503
  36.2 18.4 %collective-permute-start.7 = (f32[432,256]{1,0:T(8,128)S(1)}, f32[432,256]{1,0:T(8,128)S(1)}, u32[]{:S(2)}, u32[]{:S(2)}) collective-permute-start(f32[432,256]{1,0:T(8,128)S(1)} %get-tuple-element.36), channel_id=1, source_target_pairs={{0,2},{2,0},{4,6},{6,4},{8,10},{10,8},{12,14},{14,12},{1,3},{3,1},... | collective-permute-start | bytes 1327112 | tf_op jit(solution)/shard_map/ppermute | solution.py:503
  36.7 17.9 %collective-permute-start.8 = (f32[432,256]{1,0:T(8,128)S(1)}, f32[432,256]{1,0:T(8,128)S(1)}, u32[]{:S(2)}, u32[]{:S(2)}) collective-permute-start(f32[432,256]{1,0:T(8,128)S(1)} %get-tuple-element.37), channel_id=1, source_target_pairs={{2,4},{4,2},{6,8},{8,6},{10,12},{12,10},{3,5},{5,3},{7,9},{9,7},{1... | collective-permute-start | bytes 1327112 | tf_op jit(solution)/shard_map/ppermute | solution.py:503
  38.5 1.5 %collective-permute-start.6 = (f32[432,128]{1,0:T(8,128)S(1)}, f32[432,128]{1,0:T(8,128)S(1)}, u32[]{:S(2)}, u32[]{:S(2)}) collective-permute-start(f32[432,128]{1,0:T(8,128)S(1)} %maximum_select_fusion.mine_ref), channel_id=1, source_target_pairs={{0,1},{1,0},{2,3},{3,2},{4,5},{5,4},{6,7},{7,6},{8,9},{9,8},{10,11... | collective-permute-start | bytes 663560 | tf_op jit(solution)/shard_map/ppermute | solution.py:503
  39.3 15.4 %copy-start.3 = (f32[432,512]{1,0:T(8,128)S(1)}, f32[432,512]{1,0:T(8,128)}, u32[]{:S(2)}) copy-start(f32[432,512]{1,0:T(8,128)} %copy-done.2) | copy-start | bytes 2654212

commit v3 on v2

--- a/solution.py
+++ b/solution.py
@@ -100,8 +100,26 @@
 
 
 def neighbour_steps(p):
-    near, far = 1 - 2 * (p & 1), 2 - 2 * (p & 2)
-    return near, -near, far, -far
+    near = 1 - 2 * (p & 1)
+    return near, -near, 2 * near, -2 * near
+
+
+def relay_lanes(samp_ops, n_samp):
+    lanes = output_lanes()
+    pairs = []
+    for parity in range(2):
+        used = np.zeros((2, COUNT), bool)
+        for p in range(n_samp):
+            for k, step in enumerate((1 - 2 * parity, 2 - 4 * parity)):
+                if 0 <= p + step < n_samp:
+                    for o, (level, _, part, _, samp) in enumerate(lanes):
+                        row = samp_ops[level, part][(p + step) * (SD >> level) + samp]
+                        used[k, o] |= row[p * SD : (p + 1) * SD].any()
+        free = [o - LEVEL1 for o in range(LEVEL1, COUNT) if not used[0, o]]
+        wanted = [o for o in range(COUNT) if used[1, o]]
+        assert len(wanted) <= len(free)
+        pairs.append(list(zip(free, wanted)))
+    return pairs
 
 
 def build_constants(n_samp, n_line):
@@ -124,6 +142,13 @@
         return table
 
     size = COUNT + 5 * LANES
+    relays = relay_lanes(samp_ops, n_samp)
+    select = np.zeros((2, 2 * LANES, LANES))
+    for parity in range(2):
+        passed, moved = dict(relays[1 - parity]), dict(relays[parity])
+        for lane in range(LANES):
+            select[parity, lane, lane] = float(lane not in passed)
+            select[parity, LANES + lane, moved[lane] - LEVEL1 if lane in moved else lane] = 1.0
     line_table = np.zeros((n_line, n_line * LD, size))
     samp_table = np.zeros((n_samp, SD, size))
     line_table[:, :, :COUNT] = line_own
@@ -136,8 +161,12 @@
                     line_table[:, :, at + line * WIDE + 2 * sb + j] = line_own[:, :, source]
         at = COUNT + (2 + k) * LANES
         line_table[:, :, at : at + LANES] = line_own[:, :, LEVEL1:]
-        at = COUNT + 4 * LANES + k * FAR
-        line_table[:, :, at : at + FAR] = line_own[:, :, COUNT - FAR :]
+    at = COUNT + 4 * LANES
+    line_table[:, :, at : at + FAR] = line_own[:, :, COUNT - FAR :]
+    line_table = np.stack([line_table] * 2, 1)
+    for parity in range(2):
+        for lane, o in relays[parity]:
+            line_table[:, parity, :, COUNT + 2 * LANES + lane] = line_own[:, :, o]
     offsets = np.zeros((n_samp, n_line, 8, COUNT))
     line_sums = line_own.sum(1)
     for p in range(n_samp):
@@ -159,15 +188,28 @@
                 samp_table[p, :, at : at + LANES] = given[:, LEVEL1:]
             else:
                 assert not given[:, : COUNT - FAR].any()
-                at = COUNT + 4 * LANES + (k - 2) * FAR
-                samp_table[p, :, at : at + FAR] = given[:, COUNT - FAR :]
+                if k == 2:
+                    for lane, o in relays[p % 2]:
+                        samp_table[p, :, COUNT + 2 * LANES + lane] = given[:, o]
+                else:
+                    at = COUNT + 4 * LANES
+                    samp_table[p, :, at : at + FAR] = given[:, COUNT - FAR :]
             if 0 <= p + step < n_samp:
                 sums = reach(p + step, -step).sum(0)
                 offsets[p, :, k] = sums * line_sums
                 whole = whole + sums
         offsets[p, :, 4] = whole * line_sums
         offsets[p, :, 4] -= offsets[p, :, :4].sum(1)
-    return line_table.astype(np.float32), samp_table.astype(np.float32), offsets.astype(np.float32)
+    relayed = np.zeros((2, 1, LANES), bool)
+    for parity in range(2):
+        relayed[parity, 0, [lane for lane, _ in relays[parity]]] = True
+    return (
+        line_table.astype(np.float32),
+        samp_table.astype(np.float32),
+        offsets.astype(np.float32),
+        select.astype(np.float32),
+        relayed,
+    )
 
 
 EDGES = list(range(0, BANDS, BLOCK)) + [BANDS]
@@ -263,10 +305,15 @@
             xs[k, :, g * LANES : (g + 1) * LANES] = part
 
 
-def strip_product(line_ref, samp_ref, xs, matrix, start, width, depth):
-    samp = samp_ref[:, start : start + width]
+def strip_product(line_ref, samp_ref, xs, matrix, starts, depth):
+    width = len(starts) * LANES
+
+    def tiles_of(ref, rows):
+        return jnp.concatenate([ref[rows, start : start + LANES] for start in starts], 1)
+
+    samp = tiles_of(samp_ref, slice(None))
     for line in range(depth // SD):
-        values = samp * line_ref[line : line + 1, start : start + width]
+        values = samp * tiles_of(line_ref, slice(line, line + 1))
         for k, part in enumerate(split3(values)):
             matrix[k, line * SD : (line + 1) * SD, 0:width] = part
     return product_parts(
@@ -290,28 +337,31 @@
 FAR_HELD = -(-FAR_ROWS // 8) * 8
 
 
-def contribution_kernel(
-    where_ref, x_ref, other_ref, mean_ref, line_ref, samp_ref, near1, near2, far1, far2, xs, matrix, small
-):
+NEAR_SHALLOW, NEAR_DEEP, FAR_AT = COUNT, COUNT + 2 * LANES, COUNT + 4 * LANES
+
+
+def first_kernel(where_ref, x_ref, other_ref, mean_ref, line_ref, samp_ref, xs, near1, far, matrix, small):
     load_strip(where_ref, x_ref, other_ref, mean_ref, xs)
     run = functools.partial(strip_product, line_ref, samp_ref, xs, matrix)
-    small[...] = run(COUNT + 4 * LANES, LANES, 2 * COUNT)
-    for k, ref in enumerate((far1, far2)):
-        ref[FAR_ROWS:, :] = jnp.zeros_like(ref[FAR_ROWS:, :])
-        ref[0:FAR_ROWS, :] = repacked(small, k * FAR, FAR)
-    first = run(COUNT, 2 * LANES, SHALLOW)
-    near1[:, 0:LANES] = first[:, 0:LANES]
-    near2[:, 0:LANES] = first[:, LANES:]
-    second = run(COUNT + 2 * LANES, 2 * LANES, 2 * COUNT)
-    near1[:, LANES:] = second[:, 0:LANES]
-    near2[:, LANES:] = second[:, LANES:]
-
-
-def own_kernel(where_ref, x_ref, other_ref, mean_ref, line_ref, samp_ref, own_ref, xs, matrix):
-    load_strip(where_ref, x_ref, other_ref, mean_ref, xs)
+    near1[:, 0:LANES] = run((NEAR_SHALLOW,), SHALLOW)
+    deep = run((NEAR_DEEP, FAR_AT), 2 * COUNT)
+    near1[:, LANES:] = deep[:, 0:LANES]
+    small[...] = deep[:, LANES:]
+    far[FAR_ROWS:, :] = jnp.zeros_like(far[FAR_ROWS:, :])
+    far[0:FAR_ROWS, :] = repacked(small, 0, FAR)
+
+
+def second_kernel(xs, line_ref, samp_ref, near2, own_deep, matrix):
     run = functools.partial(strip_product, line_ref, samp_ref, xs, matrix)
-    own_ref[:, 0:LEVEL1] = run(0, LEVEL1, SHALLOW)
-    own_ref[:, LEVEL1:] = run(LEVEL1, COUNT - LEVEL1, 2 * COUNT)
+    near2[:, 0:LANES] = run((NEAR_SHALLOW + LANES,), SHALLOW)
+    deep = run((NEAR_DEEP + LANES, LEVEL1), 2 * COUNT)
+    near2[:, LANES:] = deep[:, 0:LANES]
+    own_deep[...] = deep[:, LANES:]
+
+
+def third_kernel(xs, line_ref, samp_ref, own_shallow, matrix):
+    run = functools.partial(strip_product, line_ref, samp_ref, xs, matrix)
+    own_shallow[...] = run(tuple(range(0, LEVEL1, LANES)), SHALLOW)
 
 
 def spread(value):
@@ -448,16 +498,16 @@
 
 
 def output_kernel(
-    n_line, pixels, where_ref, own_ref, dev_ref, w_ref, offset_ref, near1, near2, far_ref, *rest
+    n_line, pixels, where_ref, own_ref, deep_ref, dev_ref, w_ref, offset_ref, select_ref, near1, near2, far_ref, *rest
 ):
     (out1_ref, out2_ref, out3_ref, approx_ref), (d, small) = rest[:4], rest[4:]
     tile, samp = where_ref[0], where_ref[2]
     bit = samp % 2
     tiles = dev_ref.shape[0]
     which = lax.broadcasted_iota(jnp.int32, (tiles, COUNT), 0)
-    near, far = 1 - 2 * bit, 2 - 4 * ((samp // 2) % 2)
+    near = 1 - 2 * bit
     gains = jnp.where(which == tile, offset_ref[4:5, :], 0.0)
-    for k, step in enumerate((near, -near, far, -far)):
+    for k, step in enumerate((near, -near, 2 * near, -2 * near)):
         gains += jnp.where(which == tile + n_line * step, offset_ref[k : k + 1, :], 0.0)
     shift = product(dev_ref[:, 0:BANDS], gains, 0, 0)
     together = LANES // FAR
@@ -472,6 +522,14 @@
         for k, part in enumerate(split3(value * scale)):
             d[k, :, at : at + LANES] = part
 
+    deep = split3(jnp.concatenate([near1[:, LANES:], near2[:, LANES:]], 1))
+    select = select_ref[...].astype(jnp.bfloat16)
+    near_deep = lax.dot_general(
+        jnp.concatenate(deep, 1),
+        jnp.concatenate([select] * 3, 0),
+        (((1,), (0,)), ((), ())),
+        preferred_element_type=jnp.float32,
+    )
     bases = ((WIDE - 2) * (1 - bit), (WIDE - 2) * bit)
     for sb in range(3):
         at = sb * LANES
@@ -482,7 +540,7 @@
         keep(at, value)
     keep(
         LEVEL1,
-        own_ref[:, LEVEL1:] + shift[:, LEVEL1:] + near1[:, LANES:] + near2[:, LANES:] + small[...],
+        deep_ref[...] + shift[:, LEVEL1:] + near_deep + small[...],
     )
     for low, high in ((0, 2 * BLOCK), (2 * BLOCK, BANDS)):
         w = split3(w_ref[low:high, :high])
@@ -521,17 +579,20 @@
     return pl.pallas_call(
         kernel,
         name=name,
-        out_shape=[jax.ShapeDtypeStruct(shape, jnp.float32) for shape in shapes],
+        out_shape=[
+            shape if isinstance(shape, jax.ShapeDtypeStruct) else jax.ShapeDtypeStruct(shape, jnp.float32)
+            for shape in shapes
+        ],
         in_specs=specs,
         out_specs=[VMEM] * len(shapes),
         scratch_shapes=[pltpu.VMEM(shape, dtype) for shape, dtype in scratch],
-        compiler_params=pltpu.CompilerParams(vmem_limit_bytes=40 * 2**20),
+        compiler_params=pltpu.CompilerParams(vmem_limit_bytes=16 * 2**20),
         cost_estimate=pl.CostEstimate(flops=flops, bytes_accessed=size, transcendentals=0),
     )(*inputs)
 
 
 def local(constants, cube):
-    line_table, samp_table, offset_table = (jnp.asarray(table) for table in constants)
+    line_table, samp_table, offset_table, select_table, relayed = (jnp.asarray(table) for table in constants)
     n_samp, n_line = lax.axis_size("samp"), lax.axis_size("line")
     tiles = n_samp * n_line
     samp, line = lax.axis_index("samp"), lax.axis_index("line")
@@ -541,6 +602,9 @@
     other = permuted(x, "line", lambda i: i ^ 1)
     _, total = payload_rows(tiles)
     half, quarter = total // 2, total // 4
+    lines, samps = line_table[line, samp & 1], samp_table[samp]
+    offset, select = offset_table[samp, line], select_table[samp & 1]
+    x, lines = lax.optimization_barrier((x, lines))
     send, keep, mean = call(
         functools.partial(gram_kernel, tiles),
         "gram",
@@ -553,46 +617,51 @@
     side = ((samp >> 1) ^ (samp >> 2)) & 1
     kept = lax.dynamic_slice_in_dim(summed, side * quarter, quarter, 0)
     given = lax.dynamic_slice_in_dim(summed, (1 - side) * quarter, quarter, 0)
+
+    mean, given, other, samps = lax.optimization_barrier((mean, given, other, samps))
+    strip, near1, far = call(
+        first_kernel,
+        "first",
+        [jax.ShapeDtypeStruct((3, BANDS, 2 * COUNT), bf16), (BANDS, 2 * LANES), (FAR_HELD, LANES)],
+        [where, x, other, mean, lines, samps],
+        [((3, 2 * COUNT, 2 * LANES), bf16), ((BANDS, LANES), f32)],
+        2 * BANDS * 2 * COUNT * 3 * LANES * 6,
+    )
     kept = kept + permuted(given, "samp", lambda i: i ^ 2)
-
-    strip_scratch = [((3, BANDS, 2 * COUNT), bf16), ((3, 2 * COUNT, LEVEL1), bf16)]
-    lines, samps = line_table[line], samp_table[samp]
-    near1, near2, far1, far2 = call(
-        contribution_kernel,
-        "contributions",
-        [(BANDS, 2 * LANES)] * 2 + [(FAR_HELD, LANES)] * 2,
-        [where, x, other, mean, lines, samps],
-        strip_scratch + [((BANDS, LANES), f32)],
-        2 * BANDS * 2 * COUNT * 5 * LANES * 6,
-    )
-    kept, near1, near2 = lax.optimization_barrier((kept, near1, near2))
-    kept2 = kept + permuted(kept, "samp", lambda i: i ^ 1)
-    mean_later, _ = lax.optimization_barrier((mean, kept))
+    kept, near1, far, strip = lax.optimization_barrier((kept, near1, far, strip))
+    near2, own_deep = call(
+        second_kernel,
+        "second",
+        [(BANDS, 2 * LANES), (BANDS, LANES)],
+        [strip, lines, samps],
+        [((3, 2 * COUNT, 2 * LANES), bf16)],
+        2 * BANDS * 2 * COUNT * 3 * LANES * 6,
+    )
+    kept = kept + permuted(kept, "samp", lambda i: i ^ 1)
+    kept, near1, near2, own_deep, far, strip = lax.optimization_barrier(
+        (kept, near1, near2, own_deep, far, strip)
+    )
+    near1 = permuted(near1, "samp", lambda i: i ^ 1)
     (own,) = call(
-        own_kernel,
-        "own",
-        [(BANDS, COUNT)],
-        [where, x, other, mean_later, lines, samps],
-        strip_scratch,
-        2 * BANDS * 2 * COUNT * COUNT * 6,
-    )
-    kept, own = lax.optimization_barrier((kept2, own))
-    far = jnp.zeros_like(far2)
+        third_kernel,
+        "third",
+        [(BANDS, LEVEL1)],
+        [strip, lines, samps],
+        [((3, SHALLOW, LEVEL1), bf16)],
+        2 * BANDS * 2 * COUNT * 3 * LANES * 6,
+    )
     size = 8
     while size <= n_samp:
-        partner = mirrored(size)
-        both = permuted(jnp.concatenate([kept, far2]), "samp", partner)
-        kept = kept + both[:quarter]
-        adjacent = jnp.asarray([abs(partner(i) - i) == 2 for i in range(n_samp)])[samp]
-        far = far + jnp.where(adjacent, both[quarter:], 0.0)
+        kept = kept + permuted(kept, "samp", mirrored(size))
         size *= 2
-    both = permuted(jnp.concatenate([kept, far1]), "samp", lambda i: i ^ 2)
-    back = both[:quarter]
-    far = far + both[quarter:]
+    kept, own, far, offset, select = lax.optimization_barrier((kept, own, far, offset, select))
+    far = permuted(far, "samp", lambda i: i + 2 if i & 1 else i - 2)
+    back = permuted(kept, "samp", lambda i: i ^ 2)
     mine = jnp.where(side == 0, jnp.concatenate([kept, back]), jnp.concatenate([back, kept]))
+    mine, near1 = lax.optimization_barrier((mine, near1))
     theirs = permuted(mine, "line", lambda i: i ^ 1)
-    near1 = permuted(near1, "samp", lambda i: i ^ 1)
-    near2 = permuted(near2, "samp", lambda i: ((i + 1) ^ 1) - 1)
+    on = jnp.concatenate([jnp.zeros_like(relayed), relayed], 2)[1 - (samp & 1)]
+    near2 = permuted(jnp.where(on, near1, near2), "samp", lambda i: ((i + 1) ^ 1) - 1)
 
     w, dev = call(
         functools.partial(whiten_kernel, tiles),
@@ -600,7 +669,7 @@
         [(BANDS, BANDS), (tiles, 4 * BLOCK)],
         [where, mine, theirs],
         [((total, LANES), f32), ((BANDS, 4 * BLOCK), f32), ((2, 16, 8, LANES), f32)],
-        2 * 10**10,
+        10**8,
     )
     outs = call(
         functools.partial(output_kernel, n_line, COUNT * tiles),
@@ -611,7 +680,7 @@
             (3 * BANDS * (COUNT // 64) // LANES, LANES),
             (BANDS * (COUNT // 64) // LANES, LANES),
         ],
-        [where, own, dev, w, offset_table[samp, line], near1, near2, far],
+        [where, own, own_deep, dev, w, offset, select, near1, near2, far],
         [((3, BANDS, COUNT), bf16), ((BANDS, LANES), f32)],
         2 * BANDS * BANDS * COUNT * 6,
     )

time: 58.2 us -> 53.9 us (0.926)
  the two profiles are of different devices: /device:TPU:0 before, /device:TPU:15 now
where the time goes in v3:
time: 53.9 us; the launch traced here: 53.6 us
  Pallas kernels  25.1 us (47%)
  starting transfers between devices  16.5 us (31%)
  waiting for transfers between devices  7.02 us (13%)
  local copies, waits for them, and re-layouts  3.91 us (7%)
  between operations  0.81 us (2%)
    pallas_call x6, Pallas kernels, call(): pl.pallas_call(kernel, name=name, out_shape=[shape if isinstance(shape, j...  25.1 us
    ppermute x10, starting transfers between devices, permuted(): lax.ppermute(array, axis, [(i, partner(i)) for i in range(count) if 0 <=...  16.5 us
    ppermute x10, waiting for transfers between devices, permuted(): lax.ppermute(array, axis, [(i, partner(i)) for i in range(count) if 0 <=...  7.02 us
    squeeze x2, local copies, waits for them, and re-layouts, local(): lines, samps = (line_table[line, samp & 1], samp_table[samp])  1.95 us
    unnamed x12, local copies, waits for them, and re-layouts  1.2 us
  transfers between devices with their start and end apart: 10, of which 5 were waited for; matrix products, arithmetic and copies ran while one was open for 5% of the time, Pallas kernels for 40%

profile of v3, /device:TPU:15, one launch (start us, length us, event | category | flops | bytes accessed | tf_op | source)
XLA Modules:
  0.0 53.6 jit_solution(12398331755152750093)
XLA Ops:
  0.6 0.7 %collective-permute-start.1 = (f32[1728,128]{1,0:T(8,128)}, f32[1728,128]{1,0:T(8,128)S(1)}, u32[]{:S(2)}, u32[]{:S(2)}) collective-permute-start(f32[1728,128]{1,0:T(8,128)} %bitcast.16), channel_id=1, source_target_pairs={{0,1},{1,0},{2,3},{3,2},{4,5},{5,4},{6,7},{7,6},{8,9},{9,8},{10,11... | collective-permute-start | bytes 2654216 | tf_op jit(solution)/shard_map/ppermute | solution.py:561
  1.4 1.0 %dynamic-slice_bitcast_fusion.line_ref = f32[64,1152]{1,0:T(8,128)S(1)} fusion(f32[2,2,64,1152]{3,2,1,0:T(8,128)} %constant.34.clone, s32[]{:T(128)S(6)} %select_n.33, s32[]{:T(128)S(6)} %select_n.34), kind=kLoop, calls=%fused_computation | loop fusion | bytes 589832 | tf_op jit(solution)/shard_map/squeeze | solution.py:605
  2.4 0.1 pad_add_fusion.where_ref
  2.4 1.2 %copy-done = f32[221184]{0:T(1024)S(1)} copy-done((f32[221184]{0:T(1024)S(1)}, f32[221184]{0:T(1024)}, u32[]{:S(2)}) %copy-start) | copy-done | bytes 884760
  3.6 2.4 %gram.1 = (f32[432,128]{1,0:T(8,128)S(1)}, f32[432,128]{1,0:T(8,128)S(1)}, f32[432,128]{1,0:T(8,128)S(1)}) custom-call(s32[3]{0:T(128)S(1)} %pad_add_fusion.where_ref, f32[1728,128]{1,0:T(8,128)S(1)} %bitcast.17), custom_call_target="tpu_custom_call" | custom-call | flops 764411904 | bytes 884748 | tf_op jit(solution)/shard_map/gram/pallas_call | solution.py:579
  6.0 0.0 copy-start.1
  6.0 0.1 collective-permute-start
  6.1 1.0 %dynamic-slice_bitcast_fusion.2.samp_ref = f32[16,1152]{1,0:T(8,128)S(1)} fusion(f32[8,16,1152]{2,1,0:T(8,128)} %constant.35.clone, s32[]{:T(128)S(6)} %select_n.37), kind=kLoop, calls=%fused_computation.5 | loop fusion | bytes 147460 | tf_op jit(solution)/shard_map/squeeze | solution.py:605
  7.1 0.5 collective-permute-done
  7.6 0.0 collective-permute-done.1.other_ref
  7.6 0.2 collective-permute-start.2
  7.8 3.5 %first.1 = (bf16[3,432,1024]{2,1,0:T(8,128)(2,1)S(1)}, f32[432,256]{1,0:T(8,128)S(1)}, f32[112,128]{1,0:T(8,128)S(1)}) custom-call(s32[3]{0:T(128)S(1)} %pad_add_fusion.where_ref, f32[1728,128]{1,0:T(8,128)S(1)} %bitcast.18, f32[1728,128]{1,0:T(8,128)S(1)} %collective-permute-done.1.other_ref, f32[432,128]{1,0:T(8,128)S(1)} %get-tuple-element.47.mean_ref, ...), custom_call_target="tpu_custom_call" | custom-call | flops 2038431744 | bytes 2359308 | tf_op jit(solution)/shard_map/first/pallas_call | solution.py:579
  11.4 0.0 copy-start.2
  11.4 0.8 %collective-permute-done.2 = f32[216,128]{1,0:T(8,128)S(1)} collective-permute-done((f32[216,128]{1,0:T(8,128)S(1)}, f32[216,128]{1,0:T(8,128)S(1)}, u32[]{:S(2)}, u32[]{:S(2)}) %collective-permute-start.2) | collective-permute-done | bytes 110624 | tf_op jit(solution)/shard_map/ppermute | solution.py:561
  12.2 0.3 collective-permute-start.3
  12.5 2.7 %second.1 = (f32[432,256]{1,0:T(8,128)S(1)}, f32[432,128]{1,0:T(8,128)S(1)}) custom-call(bf16[3,432,1024]{2,1,0:T(8,128)(2,1)S(1)} %get-tuple-element.60.xs, f32[64,1152]{1,0:T(8,128)S(1)} %dynamic-slice_bitcast_fusion.line_ref, f32[16,1152]{1,0:T(8,128)S(1)} %dynamic-slice_bitcast_fusion.2.samp_ref), custom_call_target="tpu_custom_call" | custom-call | flops 2038431744 | bytes 5677056 | tf_op jit(solution)/shard_map/second/pallas_call | solution.py:579
  15.2 0.7 %collective-permute-done.3 = f32[216,128]{1,0:T(8,128)S(1)} collective-permute-done((f32[216,128]{1,0:T(8,128)S(1)}, f32[216,128]{1,0:T(8,128)S(1)}, u32[]{:S(2)}, u32[]{:S(2)}) %collective-permute-start.3) | collective-permute-done | bytes 110624 | tf_op jit(solution)/shard_map/ppermute | solution.py:561
  15.9 0.6 %collective-permute-start.6 = (f32[432,256]{1,0:T(8,128)S(1)}, f32[432,256]{1,0:T(8,128)S(1)}, u32[]{:S(2)}, u32[]{:S(2)}) collective-permute-start(f32[432,256]{1,0:T(8,128)S(1)} %get-tuple-element.65), channel_id=1, source_target_pairs={{0,2},{2,0},{4,6},{6,4},{8,10},{10,8},{12,14},{14,12},{1,3},{3,1},... | collective-permute-start | bytes 1327112 | tf_op jit(solution)/shard_map/ppermute | solution.py:561
  16.5 0.7 %dynamic-slice_bitcast_fusion.3.offset_ref = f32[8,512]{1,0:T(8,128)S(1)} fusion(f32[8,2,8,512]{3,2,1,0:T(8,128)} %constant.36.clone, s32[]{:T(128)S(6)} %select_n.37, s32[]{:T(128)S(6)} %select_n.33), kind=kLoop, calls=%fused_computation.6 | loop fusion | bytes 32776 | tf_op jit(solution)/shard_map/squeeze | solution.py:606
  17.2 1.7 %collective-permute-start.4 = (f32[216,128]{1,0:T(8,128)S(1)}, f32[216,128]{1,0:T(8,128)S(1)}, u32[]{:S(2)}, u32[]{:S(2)}) collective-permute-start(f32[216,128]{1,0:T(8,128)S(1)} %add.45), channel_id=1, source_target_pairs={{0,12},{2,14},{4,8},{6,10},{8,4},{10,6},{12,0},{14,2},{1,13},{3,15... | collective-permute-start | bytes 331784 | tf_op jit(solution)/shard_map/ppermute | solution.py:561
  18.9 2.0 %third.1.own_ref = f32[432,384]{1,0:T(8,128)S(1)} custom-call(bf16[3,432,1024]{2,1,0:T(8,128)(2,1)S(1)} %get-tuple-element.60.xs, f32[64,1152]{1,0:T(8,128)S(1)} %dynamic-slice_bitcast_fusion.line_ref, f32[16,1152]{1,0:T(8,128)S(1)} %dynamic-slice_bitcast_fusion.2.samp_ref), custom_call_target="tpu_custom_call" | custom-call | flops 2038431744 | bytes 5677056 | tf_op jit(solution)/shard_map/third/pallas_call | solution.py:579
  20.9 0.0 copy-start.3
  20.9 1.6 %collective-permute-done.4 = f32[216,128]{1,0:T(8,128)S(1)} collective-permute-done((f32[216,128]{1,0:T(8,128)S(1)}, f32[216,128]{1,0:T(8,128)S(1)}, u32[]{:S(2)}, u32[]{:S(2)}) %collective-permute-start.4) | collective-permute-done | bytes 110624 | tf_op jit(solution)/shard_map/ppermute | solution.py:561
  22.6 0.8 %collective-permute-start.5 = (f32[216,128]{1,0:T(8,128)S(1)}, f32[216,128]{1,0:T(8,128)S(1)}, u32[]{:S(2)}, u32[]{:S(2)}) collective-permute-start(f32[216,128]{1,0:T(8,128)S(1)} %add.46), channel_id=1, source_target_pairs={{0,4},{2,6},{4,0},{6,2},{8,12},{10,14},{12,8},{14,10},{1,5},{3,7},... | collective-permute-start | bytes 331784 | tf_op jit(solution)/shard_map/ppermute | solution.py:561
  23.4 3.4 %collective-permute-done.5 = f32[216,128]{1,0:T(8,128)S(1)} collective-permute-done((f32[216,128]{1,0:T(8,128)S(1)}, f32[216,128]{1,0:T(8,128)S(1)}, u32[]{:S(2)}, u32[]{:S(2)}) %collective-permute-start.5) | collective-permute-done | bytes 110624 | tf_op jit(solution)/shard_map/ppermute | solution.py:561
  26.9 0.0 collective-permute-done.6.near1
  26.9 0.1 broadcast_select_fusion
  26.9 3.4 %collective-permute-start.8 = (f32[432,256]{1,0:T(8,128)S(1)}, f32[432,256]{1,0:T(8,128)S(1)}, u32[]{:S(2)}, u32[]{:S(2)}) collective-permute-start(f32[432,256]{1,0:T(8,128)S(1)} %broadcast_select_fusion), channel_id=1, source_target_pairs={{2,4},{4,2},{6,8},{8,6},{10,12},{12,10},{3,5},{5,3},{7,9},{9,7},{1... | collective-permute-start | bytes 1327112 | tf_op jit(solution)/shard_map/ppermute | solution.py:561
  30.4 4.8 %collective-permute-start.7 = (f32[432,128]{1,0:T(8,128)S(1)}, f32[432,128]{1,0:T(8,128)S(1)}, u32[]{:S(2)}, u32[]{:S(2)}) collective-permute-start(f32[432,128]{1,0:T(8,128)S(1)} %maximum_select_fusion.mine_ref), channel_id=1, source_target_pairs={{0,1},{1,0},{2,3},{3,2},{4,5},{5,4},{6,7},{7,6},{8,9},{9,8},{10,11... | collective-permute-start | bytes 663560 | tf_op jit(solution)/shard_map/ppermute | solution.py:561
  35.2 3.8 %collective-permute-start.9 = (f32[112,128]{1,0:T(8,128)S(1)}, f32[112,128]{1,0:T(8,128)S(1)}, u32[]{:S(2)}, u32[]{:S(2)}) collective-permute-start(f32[112,128]{1,0:T(8,128)S(1)} %copy-done.3), channel_id=1, source_target_pairs={{2,6},{4,0},{6,10},{8,4},{10,14},{12,8},{3,7},{5,1},{7,11},{9,5},{... | collective-permute-start | bytes 172040 | tf_op jit(solution)/shard_map/ppermute | solution.py:561
  39.0 11.1 %whiten.1 = (f32[432,432]{1,0:T(8,128)S(1)}, f32[16,512]{1,0:T(8,128)S(1)}) custom-call(s32[3]{0:T(128)S(1)} %pad_add_fusion.where_ref, f32[432,128]{1,0:T(8,128)S(1)} %maximum_select_fusion.mine_ref, f32[432,128]{1,0:T(8,128)S(1)} %collective-permute-done.7.theirs_ref), custom_call_target="tpu_custom_call" | custom-call | flops 100000000 | bytes 442380 | tf_op jit(solution)/shard_map/whiten/pallas_call | solution.py:579
  50.1 3.4 %outputs.1 = (f32[1296,128]{1,0:T(8,128)}, f32[324,128]{1,0:T(8,128)}, f32[81,128]{1,0:T(8,128)}, f32[27,128]{1,0:T(8,128)}) custom-call(s32[3]{0:T(128)S(1)} %pad_add_fusion.where_ref, f32[432,384]{1,0:T(8,128)S(1)} %third.1.own_ref, f32[432,128]{1,0:T(8,128)S(1)} %get-tuple-element.63.deep_ref, f32[16,512]{1,0:T(8,128)S(1)} %get-tuple-element.67.dev_ref, ...), custom_call_target="tpu_custom_call" | custom-call | flops 1146617856 | bytes 2753548 | tf_op jit(solution)/shard_map/outputs/pallas_call | solution.py:579
  (19 shorter events, 0.2 us)
Async XLA Ops:
  0.6 7.0 %collective-permute-start.1 = (f32[1728,128]{1,0:T(8,128)}, f32[1728,128]{1,0:T(8,128)S(1)}, u32[]{:S(2)}, u32[]{:S(2)}) collective-permute-start(f32[1728,128]{1,0:T(8,128)} %bitcast.16), channel_id=1, source_target_pairs={{0,1},{1,0},{2,3},{3,2},{4,5},{5,4},{6,7},{7,6},{8,9},{9,8},{10,11... | collective-permute-start | bytes 2654216 | tf_op jit(solution)/shard_map/ppermute | solution.py:561
  2.4 1.2 %copy-start = (f32[221184]{0:T(1024)S(1)}, f32[221184]{0:T(1024)}, u32[]{:S(2)}) copy-start(f32[221184]{0:T(1024)} %param.6) | copy-start | bytes 2654212
  3.6 2.5 %copy-start.4 = (f32[2,256,128]{2,1,0:T(8,128)S(1)}, f32[2,256,128]{2,1,0:T(8,128)}, u32[]{:S(2)}) copy-start(f32[2,256,128]{2,1,0:T(8,128)} %constant.37.clone) | copy-start | bytes 786436
  6.0 1.9 %copy-start.1 = (f32[221184]{0:T(1024)S(1)}, f32[221184]{0:T(1024)}, u32[]{:S(2)}) copy-start(f32[221184]{0:T(1024)} %param.6) | copy-start | bytes 2654212
  6.0 1.5 %collective-permute-start = (f32[432,128]{1,0:T(8,128)S(1)}, f32[432,128]{1,0:T(8,128)S(1)}, u32[]{:S(2)}, u32[]{:S(2)}) collective-permute-start(f32[432,128]{1,0:T(8,128)S(1)} %get-tuple-element.43), channel_id=1, source_target_pairs={{0,1},{1,0},{2,3},{3,2},{4,5},{5,4},{6,7},{7,6},{8,9},{9,8},{10,11... | collective-permute-start | bytes 663560 | tf_op jit(solution)/shard_map/ppermute | solution.py:561
  7.6 4.6 %collective-permute-start.2 = (f32[216,128]{1,0:T(8,128)S(1)}, f32[216,128]{1,0:T(8,128)S(1)}, u32[]{:S(2)}, u32[]{:S(2)}) collective-permute-start(f32[216,128]{1,0:T(8,128)S(1)} %constant_dynamic-slice_fusion), channel_id=1, source_target_pairs={{0,4},{2,6},{4,0},{6,2},{8,12},{10,14},{12,8},{14,10},{1,5},{3,7},... | collective-permute-start | bytes 331784 | tf_op jit(solution)/shard_map/ppermute | solution.py:561
  11.4 3.8 %copy-start.2 = (f32[112,128]{1,0:T(8,128)}, f32[112,128]{1,0:T(8,128)S(1)}, u32[]{:S(2)}) copy-start(f32[112,128]{1,0:T(8,128)S(1)} %get-tuple-element.73) | copy-start | bytes 172036
  12.2 3.7 %collective-permute-start.3 = (f32[216,128]{1,0:T(8,128)S(1)}, f32[216,128]{1,0:T(8,128)S(1)}, u32[]{:S(2)}, u32[]{:S(2)}) collective-permute-start(f32[216,128]{1,0:T(8,128)S(1)} %dynamic-slice_add_fusion), channel_id=1, source_target_pairs={{0,2},{2,0},{4,6},{6,4},{8,10},{10,8},{12,14},{14,12},{1,3},{3,1},... | collective-permute-start | bytes 331784 | tf_op jit(solution)/shard_map/ppermute | solution.py:561
  15.9 11.0 %collective-permute-start.6 = (f32[432,256]{1,0:T(8,128)S(1)}, f32[432,256]{1,0:T(8,128)S(1)}, u32[]{:S(2)}, u32[]{:S(2)}) collective-permute-start(f32[432,256]{1,0:T(8,128)S(1)} %get-tuple-element.65), channel_id=1, source_target_pairs={{0,2},{2,0},{4,6},{6,4},{8,10},{10,8},{12,14},{14,12},{1,3},{3,1},... | collective-permute-start | bytes 1327112 | tf_op jit(solution)/shard_map/ppermute | solution.py:561
  17.2 6.1 %copy-start.5 = (pred[2,1,256]{2,1,0:T(4,128)(4,1)S(1)}, pred[2,1,256]{2,1,0:T(4,128)(4,1)}, u32[]{:S(2)}) copy-start(pred[2,1,256]{2,1,0:T(4,128)(4,1)} %constant.41) | copy-start | bytes 1540
  17.2 5.3 %collective-permute-start.4 = (f32[216,128]{1,0:T(8,128)S(1)}, f32[216,128]{1,0:T(8,128)S(1)}, u32[]{:S(2)}, u32[]{:S(2)}) collective-permute-start(f32[216,128]{1,0:T(8,128)S(1)} %add.45), channel_id=1, source_target_pairs={{0,12},{2,14},{4,8},{6,10},{8,4},{10,6},{12,0},{14,2},{1,13},{3,15... | collective-permute-start | bytes 331784 | tf_op jit(solution)/shard_map/ppermute | solution.py:561
  20.9 14.3 %copy-start.3 = (f32[112,128]{1,0:T(8,128)S(1)}, f32[112,128]{1,0:T(8,128)}, u32[]{:S(2)}) copy-start(f32[112,128]{1,0:T(8,128)} %copy-done.2) | copy-start | bytes 172036
  22.6 4.3 %collective-permute-start.5 = (f32[216,128]{1,0:T(8,128)S(1)}, f32[216,128]{1,0:T(8,128)S(1)}, u32[]{:S(2)}, u32[]{:S(2)}) collective-permute-start(f32[216,128]{1,0:T(8,128)S(1)} %add.46), channel_id=1, source_target_pairs={{0,4},{2,6},{4,0},{6,2},{8,12},{10,14},{12,8},{14,10},{1,5},{3,7},... | collective-permute-start | bytes 331784 | tf_op jit(solution)/shard_map/ppermute | solution.py:561
  26.9 23.2 %collective-permute-start.8 = (f32[432,256]{1,0:T(8,128)S(1)}, f32[432,256]{1,0:T(8,128)S(1)}, u32[]{:S(2)}, u32[]{:S(2)}) collective-permute-start(f32[432,256]{1,0:T(8,128)S(1)} %broadcast_select_fusion), channel_id=1, source_target_pairs={{2,4},{4,2},{6,8},{8,6},{10,12},{12,10},{3,5},{5,3},{7,9},{9,7},{1... | collective-permute-start | bytes 1327112 | tf_op jit(solution)/shard_map/ppermute | solution.py:561
  30.4 8.6 %collective-permute-start.7 = (f32[432,128]{1,0:T(8,128)S(1)}, f32[432,128]{1,0:T(8,128)S(1)}, u32[]{:S(2)}, u32[]{:S(2)}) collective-permute-start(f32[432,128]{1,0:T(8,128)S(1)} %maximum_select_fusion.mine_ref), channel_id=1, source_target_pairs={{0,1},{1,0},{2,3},{3,2},{4,5},{5,4},{6,7},{7,6},{8,9},{9,8},{10,11... | collective-permute-start | bytes 663560 | tf_op jit(solution)/shard_map/ppermute | solution.py:561
  35.2 15.0 %collective-permute-start.9 = (f32[112,128]{1,0:T(8,128)S(1)}, f32[112,128]{1,0:T(8,128)S(1)}, u32[]{:S(2)}, u32[]{:S(2)}) collective-permute-start(f32[112,128]{1,0:T(8,128)S(1)} %copy-done.3), channel_id=1, source_target_pairs={{2,6},{4,0},{6,10},{8,4},{10,14},{12,8},{3,7},{5,1},{7,11},{9,5},{... | collective-permute-start | bytes 172040 | tf_op jit(solution)/shard_map/ppermute | solution.py:561

commit v4 on v3

--- a/solution.py
+++ b/solution.py
@@ -483,26 +483,41 @@
             (rows == cols)[:height], load, 0.0
         )
     w_ref[...] = jnp.zeros_like(w_ref)
+    square = a[0:BLOCK, 0:BLOCK]
     for k in range(4):
         low, high = EDGES[k], EDGES[k + 1]
-        groups = [a[low + 8 * g : low + 8 * g + 8, low : low + BLOCK] for g in range((high - low) // 8)]
+        groups = [square[8 * g : 8 * g + 8, :] for g in range((high - low) // 8)]
         m = jnp.concatenate(inverse_factor(groups, held), 0)[:, : high - low]
+        parts = split3(m)
+        if high < BANDS:
+            end = EDGES[k + 2]
+            factor = split3(product_parts(split3(a[high:end, low:high]), parts, 1, 1))
+            update = product_parts(factor, factor, 1, 1)
+            square = a[high:end, high : high + BLOCK]
+            if end - high == BLOCK:
+                square = square - update
+            else:
+                square = jnp.concatenate([square[:, : end - high] - update, square[:, end - high :]], 1)
         if k:
-            w_ref[low:high, :low] = product(m, w_ref[low:high, :low], 1, 0)
+            w_ref[low:high, :low] = product_parts(parts, split3(w_ref[low:high, :low]), 1, 0)
         w_ref[low:high, low:high] = m
         if high < BANDS:
-            parts = split3(m)
-            factor = split3(product_parts(split3(a[high:, low:high]), parts, 1, 1))
-            a[high:, high:BANDS] = a[high:, high:BANDS] - product_parts(factor, factor, 1, 1)
-            w_ref[high:, :high] = w_ref[high:, :high] - product_parts(factor, split3(w_ref[low:high, :high]), 1, 0)
+            row = split3(w_ref[low:high, :high])
+            w_ref[high:end, :high] = w_ref[high:end, :high] - product_parts(factor, row, 1, 0)
+            if end < BANDS:
+                below = split3(product_parts(split3(a[end:, low:high]), parts, 1, 1))
+                a[end:, high:end] = a[end:, high:end] - product_parts(below, factor, 1, 1)
+                a[end:, end:BANDS] = a[end:, end:BANDS] - product_parts(below, below, 1, 1)
+                w_ref[end:, :high] = w_ref[end:, :high] - product_parts(below, row, 1, 0)
 
 
 def output_kernel(
-    n_line, pixels, where_ref, own_ref, deep_ref, dev_ref, w_ref, offset_ref, select_ref, near1, near2, far_ref, *rest
+    n_line, pixels, where_ref, own_ref, deep_ref, dev_ref, w_ref, offsets_ref, selects_ref, near1, near2, far_ref, *rest
 ):
     (out1_ref, out2_ref, out3_ref, approx_ref), (d, small) = rest[:4], rest[4:]
-    tile, samp = where_ref[0], where_ref[2]
+    tile, line, samp = where_ref[0], where_ref[1], where_ref[2]
     bit = samp % 2
+    offset_ref, select_ref = offsets_ref.at[samp, line], selects_ref.at[bit]
     tiles = dev_ref.shape[0]
     which = lax.broadcasted_iota(jnp.int32, (tiles, COUNT), 0)
     near = 1 - 2 * bit
@@ -603,8 +618,6 @@
     _, total = payload_rows(tiles)
     half, quarter = total // 2, total // 4
     lines, samps = line_table[line, samp & 1], samp_table[samp]
-    offset, select = offset_table[samp, line], select_table[samp & 1]
-    x, lines = lax.optimization_barrier((x, lines))
     send, keep, mean = call(
         functools.partial(gram_kernel, tiles),
         "gram",
@@ -618,7 +631,7 @@
     kept = lax.dynamic_slice_in_dim(summed, side * quarter, quarter, 0)
     given = lax.dynamic_slice_in_dim(summed, (1 - side) * quarter, quarter, 0)
 
-    mean, given, other, samps = lax.optimization_barrier((mean, given, other, samps))
+    mean, given, other, samps, lines = lax.optimization_barrier((mean, given, other, samps, lines))
     strip, near1, far = call(
         first_kernel,
         "first",
@@ -654,14 +667,13 @@
     while size <= n_samp:
         kept = kept + permuted(kept, "samp", mirrored(size))
         size *= 2
-    kept, own, far, offset, select = lax.optimization_barrier((kept, own, far, offset, select))
-    far = permuted(far, "samp", lambda i: i + 2 if i & 1 else i - 2)
+    kept, own, far = lax.optimization_barrier((kept, own, far))
+    far = permuted(far, "samp", lambda i: min(i + 2, n_samp - 2 + (n_samp - 1 > i) * 1) if i & 1 else max(i - 2, int(i == 0)))
     back = permuted(kept, "samp", lambda i: i ^ 2)
     mine = jnp.where(side == 0, jnp.concatenate([kept, back]), jnp.concatenate([back, kept]))
-    mine, near1 = lax.optimization_barrier((mine, near1))
     theirs = permuted(mine, "line", lambda i: i ^ 1)
     on = jnp.concatenate([jnp.zeros_like(relayed), relayed], 2)[1 - (samp & 1)]
-    near2 = permuted(jnp.where(on, near1, near2), "samp", lambda i: ((i + 1) ^ 1) - 1)
+    near2 = permuted(jnp.where(on, near1, near2), "samp", lambda i: min(max(((i + 1) ^ 1) - 1, 0), n_samp - 1))
 
     w, dev = call(
         functools.partial(whiten_kernel, tiles),
@@ -680,7 +692,7 @@
             (3 * BANDS * (COUNT // 64) // LANES, LANES),
             (BANDS * (COUNT // 64) // LANES, LANES),
         ],
-        [where, own, own_deep, dev, w, offset, select, near1, near2, far],
+        [where, own, own_deep, dev, w, offset_table, select_table, near1, near2, far],
         [((3, BANDS, COUNT), bf16), ((BANDS, LANES), f32)],
         2 * BANDS * BANDS * COUNT * 6,
     )

time: 53.9 us -> 49.8 us (0.924)
  the two profiles are of different devices: /device:TPU:15 before, /device:TPU:0 now
where the time goes in v4:
time: 49.8 us; the launch traced here: 49.5 us
  Pallas kernels  24.8 us (50%)
  starting transfers between devices  13.3 us (27%)
  local copies, waits for them, and re-layouts  4.94 us (10%)
  waiting for transfers between devices  4.51 us (9%)
  other arithmetic  1.19 us (2%)
  between operations  0.84 us (2%)
    pallas_call x6, Pallas kernels, call(): pl.pallas_call(kernel, name=name, out_shape=[shape if isinstance(shape, j...  24.8 us
    ppermute x10, starting transfers between devices, permuted(): lax.ppermute(array, axis, [(i, partner(i)) for i in range(count) if 0 <=...  13.3 us
    ppermute x10, waiting for transfers between devices, permuted(): lax.ppermute(array, axis, [(i, partner(i)) for i in range(count) if 0 <=...  4.51 us
    unnamed x14, local copies, waits for them, and re-layouts  2.95 us
    squeeze x2, local copies, waits for them, and re-layouts, local(): lines, samps = (line_table[line, samp & 1], samp_table[samp])  1.95 us
  transfers between devices with their start and end apart: 10, of which 3 were waited for; matrix products, arithmetic and copies ran while one was open for 6% of the time, Pallas kernels for 43%

profile of v4, /device:TPU:0, one launch (start us, length us, event | category | flops | bytes accessed | tf_op | source)
XLA Modules:
  0.0 49.5 jit_solution(9293620219193002711)
XLA Ops:
  0.6 0.5 %collective-permute-start.1 = (f32[1728,128]{1,0:T(8,128)}, f32[1728,128]{1,0:T(8,128)S(1)}, u32[]{:S(2)}, u32[]{:S(2)}) collective-permute-start(f32[1728,128]{1,0:T(8,128)} %bitcast.12), channel_id=1, source_target_pairs={{0,1},{1,0},{2,3},{3,2},{4,5},{5,4},{6,7},{7,6},{8,9},{9,8},{10,11... | collective-permute-start | bytes 2654216 | tf_op jit(solution)/shard_map/ppermute | solution.py:576
  1.1 0.1 pad_add_fusion.where_ref
  1.2 1.2 %copy-done = f32[221184]{0:T(1024)S(1)} copy-done((f32[221184]{0:T(1024)S(1)}, f32[221184]{0:T(1024)}, u32[]{:S(2)}) %copy-start) | copy-done | bytes 884760
  2.4 2.4 %gram.1 = (f32[432,128]{1,0:T(8,128)S(1)}, f32[432,128]{1,0:T(8,128)S(1)}, f32[432,128]{1,0:T(8,128)S(1)}) custom-call(s32[3]{0:T(128)S(1)} %pad_add_fusion.where_ref, f32[1728,128]{1,0:T(8,128)S(1)} %bitcast.13), custom_call_target="tpu_custom_call" | custom-call | flops 764411904 | bytes 884748 | tf_op jit(solution)/shard_map/gram/pallas_call | solution.py:594
  4.8 0.0 copy-start.1
  4.8 0.1 collective-permute-start
  4.9 1.1 %dynamic-slice_bitcast_fusion.line_ref = f32[64,1152]{1,0:T(8,128)S(1)} fusion(f32[2,2,64,1152]{3,2,1,0:T(8,128)} %constant.34.clone, s32[]{:T(128)S(6)} %select_n.33, s32[]{:T(128)S(6)} %select_n.34), kind=kLoop, calls=%fused_computation | loop fusion | bytes 589832 | tf_op jit(solution)/shard_map/squeeze | solution.py:620
  6.0 0.9 %dynamic-slice_bitcast_fusion.1.samp_ref = f32[16,1152]{1,0:T(8,128)S(1)} fusion(f32[8,16,1152]{2,1,0:T(8,128)} %constant.35.clone, s32[]{:T(128)S(6)} %select_n.32), kind=kLoop, calls=%fused_computation.4 | loop fusion | bytes 147460 | tf_op jit(solution)/shard_map/squeeze | solution.py:620
  6.9 0.0 collective-permute-done.1.other_ref
  6.9 3.0 %collective-permute-start.2 = (f32[216,128]{1,0:T(8,128)S(1)}, f32[216,128]{1,0:T(8,128)S(1)}, u32[]{:S(2)}, u32[]{:S(2)}) collective-permute-start(f32[216,128]{1,0:T(8,128)S(1)} %constant_dynamic-slice_fusion), channel_id=1, source_target_pairs={{0,4},{2,6},{4,0},{6,2},{8,12},{10,14},{12,8},{14,10},{1,5},{3,7},... | collective-permute-start | bytes 331784 | tf_op jit(solution)/shard_map/ppermute | solution.py:576
  9.9 3.5 %first.1 = (bf16[3,432,1024]{2,1,0:T(8,128)(2,1)S(1)}, f32[432,256]{1,0:T(8,128)S(1)}, f32[112,128]{1,0:T(8,128)S(1)}) custom-call(s32[3]{0:T(128)S(1)} %pad_add_fusion.where_ref, f32[1728,128]{1,0:T(8,128)S(1)} %bitcast.14, f32[1728,128]{1,0:T(8,128)S(1)} %collective-permute-done.1.other_ref, f32[432,128]{1,0:T(8,128)S(1)} %get-tuple-element.41.mean_ref, ...), custom_call_target="tpu_custom_call" | custom-call | flops 2038431744 | bytes 2359308 | tf_op jit(solution)/shard_map/first/pallas_call | solution.py:594
  13.5 0.0 copy-start.6
  13.5 1.6 %collective-permute-start.3 = (f32[216,128]{1,0:T(8,128)S(1)}, f32[216,128]{1,0:T(8,128)S(1)}, u32[]{:S(2)}, u32[]{:S(2)}) collective-permute-start(f32[216,128]{1,0:T(8,128)S(1)} %dynamic-slice_add_fusion), channel_id=1, source_target_pairs={{0,2},{2,0},{4,6},{6,4},{8,10},{10,8},{12,14},{14,12},{1,3},{3,1},... | collective-permute-start | bytes 331784 | tf_op jit(solution)/shard_map/ppermute | solution.py:576
  15.1 2.7 %second.1 = (f32[432,256]{1,0:T(8,128)S(1)}, f32[432,128]{1,0:T(8,128)S(1)}) custom-call(bf16[3,432,1024]{2,1,0:T(8,128)(2,1)S(1)} %get-tuple-element.54.xs, f32[64,1152]{1,0:T(8,128)S(1)} %dynamic-slice_bitcast_fusion.line_ref, f32[16,1152]{1,0:T(8,128)S(1)} %dynamic-slice_bitcast_fusion.1.samp_ref), custom_call_target="tpu_custom_call" | custom-call | flops 2038431744 | bytes 5677056 | tf_op jit(solution)/shard_map/second/pallas_call | solution.py:594
  17.8 0.6 %collective-permute-done.3 = f32[216,128]{1,0:T(8,128)S(1)} collective-permute-done((f32[216,128]{1,0:T(8,128)S(1)}, f32[216,128]{1,0:T(8,128)S(1)}, u32[]{:S(2)}, u32[]{:S(2)}) %collective-permute-start.3) | collective-permute-done | bytes 110624 | tf_op jit(solution)/shard_map/ppermute | solution.py:576
  18.4 1.6 %collective-permute-start.7 = (f32[432,256]{1,0:T(8,128)S(1)}, f32[432,256]{1,0:T(8,128)S(1)}, u32[]{:S(2)}, u32[]{:S(2)}) collective-permute-start(f32[432,256]{1,0:T(8,128)S(1)} %get-tuple-element.61), channel_id=1, source_target_pairs={{0,2},{2,0},{4,6},{6,4},{8,10},{10,8},{12,14},{14,12},{1,3},{3,1},... | collective-permute-start | bytes 1327112 | tf_op jit(solution)/shard_map/ppermute | solution.py:576
  20.0 3.6 %collective-permute-start.4 = (f32[216,128]{1,0:T(8,128)S(1)}, f32[216,128]{1,0:T(8,128)S(1)}, u32[]{:S(2)}, u32[]{:S(2)}) collective-permute-start(f32[216,128]{1,0:T(8,128)S(1)} %add.42), channel_id=1, source_target_pairs={{0,12},{2,14},{4,8},{6,10},{8,4},{10,6},{12,0},{14,2},{1,13},{3,15... | collective-permute-start | bytes 331784 | tf_op jit(solution)/shard_map/ppermute | solution.py:576
  23.6 1.7 %copy-done.5 = bf16[3,432,1024]{2,1,0:T(8,128)(2,1)S(1)} copy-done((bf16[3,432,1024]{2,1,0:T(8,128)(2,1)S(1)}, bf16[3,432,1024]{2,1,0:T(8,128)(2,1)}, u32[]{:S(2)}) %copy-start.5) | copy-done | bytes 2654232
  25.3 2.0 %third.1.own_ref = f32[432,384]{1,0:T(8,128)S(1)} custom-call(bf16[3,432,1024]{2,1,0:T(8,128)(2,1)S(1)} %copy-done.5, f32[64,1152]{1,0:T(8,128)S(1)} %dynamic-slice_bitcast_fusion.line_ref, f32[16,1152]{1,0:T(8,128)S(1)} %dynamic-slice_bitcast_fusion.1.samp_ref), custom_call_target="tpu_custom_call" | custom-call | flops 2038431744 | bytes 5677056 | tf_op jit(solution)/shard_map/third/pallas_call | solution.py:594
  27.3 0.0 collective-permute-done.4
  27.3 0.0 copy-start.2
  27.3 0.0 copy-start.3
  27.3 0.2 collective-permute-start.5
  27.6 1.9 %collective-permute-done.7.near1 = f32[432,256]{1,0:T(8,128)S(1)} collective-permute-done((f32[432,256]{1,0:T(8,128)S(1)}, f32[432,256]{1,0:T(8,128)S(1)}, u32[]{:S(2)}, u32[]{:S(2)}) %collective-permute-start.7) | collective-permute-done | bytes 442400 | tf_op jit(solution)/shard_map/ppermute | solution.py:576
  29.5 0.1 broadcast_select_fusion
  29.6 0.7 %collective-permute-start.8 = (f32[432,256]{1,0:T(8,128)S(1)}, f32[432,256]{1,0:T(8,128)S(1)}, u32[]{:S(2)}, u32[]{:S(2)}) collective-permute-start(f32[432,256]{1,0:T(8,128)S(1)} %broadcast_select_fusion), channel_id=1, source_target_pairs={{0,0},{2,4},{4,2},{6,8},{8,6},{10,12},{12,10},{14,14},{1,1},{3,5},... | collective-permute-start | bytes 1327112 | tf_op jit(solution)/shard_map/ppermute | solution.py:576
  30.3 2.0 %collective-permute-done.5 = f32[216,128]{1,0:T(8,128)} collective-permute-done((f32[216,128]{1,0:T(8,128)S(1)}, f32[216,128]{1,0:T(8,128)}, u32[]{:S(2)}, u32[]{:S(2)}) %collective-permute-start.5) | collective-permute-done | bytes 110624 | tf_op jit(solution)/shard_map/ppermute | solution.py:576
  32.3 1.0 %maximum_select_fusion.mine_ref = f32[432,128]{1,0:T(8,128)S(1)} fusion(f32[216,128]{1,0:T(8,128)} %collective-permute-done.5, f32[216,128]{1,0:T(8,128)S(1)} %add.43, pred[]{:T(512)S(6)} %eq.3), kind=kLoop, calls=%fused_computation.1 | loop fusion | flops 165888 | bytes 442369 | tf_op jit(solution)/shard_map/jit(_where)/select_n | solution.py:673
  33.2 0.1 collective-permute-start.6
  33.3 1.9 %collective-permute-start.9 = (f32[112,128]{1,0:T(8,128)S(1)}, f32[112,128]{1,0:T(8,128)S(1)}, u32[]{:S(2)}, u32[]{:S(2)}) collective-permute-start(f32[112,128]{1,0:T(8,128)S(1)} %get-tuple-element.63), channel_id=1, source_target_pairs={{0,2},{2,6},{4,0},{6,10},{8,4},{10,14},{12,8},{14,12},{1,3},{3,7},... | collective-permute-start | bytes 172040 | tf_op jit(solution)/shard_map/ppermute | solution.py:576
  35.2 10.8 %whiten.1 = (f32[432,432]{1,0:T(8,128)S(1)}, f32[16,512]{1,0:T(8,128)S(1)}) custom-call(s32[3]{0:T(128)S(1)} %pad_add_fusion.where_ref, f32[432,128]{1,0:T(8,128)S(1)} %maximum_select_fusion.mine_ref, f32[432,128]{1,0:T(8,128)S(1)} %collective-permute-done.6.theirs_ref), custom_call_target="tpu_custom_call" | custom-call | flops 100000000 | bytes 442380 | tf_op jit(solution)/shard_map/whiten/pallas_call | solution.py:594
  46.1 3.4 %outputs.1 = (f32[1296,128]{1,0:T(8,128)}, f32[324,128]{1,0:T(8,128)}, f32[81,128]{1,0:T(8,128)}, f32[27,128]{1,0:T(8,128)}) custom-call(s32[3]{0:T(128)S(1)} %pad_add_fusion.where_ref, f32[432,384]{1,0:T(8,128)S(1)} %third.1.own_ref, f32[432,128]{1,0:T(8,128)S(1)} %get-tuple-element.57.deep_ref, f32[16,512]{1,0:T(8,128)S(1)} %get-tuple-element.59.dev_ref, ...), custom_call_target="tpu_custom_call" | custom-call | flops 1146617856 | bytes 3130380 | tf_op jit(solution)/shard_map/outputs/pallas_call | solution.py:594
  (19 shorter events, 0.1 us)
Async XLA Ops:
  0.6 6.3 %collective-permute-start.1 = (f32[1728,128]{1,0:T(8,128)}, f32[1728,128]{1,0:T(8,128)S(1)}, u32[]{:S(2)}, u32[]{:S(2)}) collective-permute-start(f32[1728,128]{1,0:T(8,128)} %bitcast.12), channel_id=1, source_target_pairs={{0,1},{1,0},{2,3},{3,2},{4,5},{5,4},{6,7},{7,6},{8,9},{9,8},{10,11... | collective-permute-start | bytes 2654216 | tf_op jit(solution)/shard_map/ppermute | solution.py:576
  1.2 1.2 %copy-start = (f32[221184]{0:T(1024)S(1)}, f32[221184]{0:T(1024)}, u32[]{:S(2)}) copy-start(f32[221184]{0:T(1024)} %param.6) | copy-start | bytes 2654212
  4.8 5.2 %copy-start.1 = (f32[221184]{0:T(1024)S(1)}, f32[221184]{0:T(1024)}, u32[]{:S(2)}) copy-start(f32[221184]{0:T(1024)} %param.6) | copy-start | bytes 2654212
  4.8 2.1 %collective-permute-start = (f32[432,128]{1,0:T(8,128)S(1)}, f32[432,128]{1,0:T(8,128)S(1)}, u32[]{:S(2)}, u32[]{:S(2)}) collective-permute-start(f32[432,128]{1,0:T(8,128)S(1)} %get-tuple-element.37), channel_id=1, source_target_pairs={{0,1},{1,0},{2,3},{3,2},{4,5},{5,4},{6,7},{7,6},{8,9},{9,8},{10,11... | collective-permute-start | bytes 663560 | tf_op jit(solution)/shard_map/ppermute | solution.py:576
  6.9 6.6 %collective-permute-start.2 = (f32[216,128]{1,0:T(8,128)S(1)}, f32[216,128]{1,0:T(8,128)S(1)}, u32[]{:S(2)}, u32[]{:S(2)}) collective-permute-start(f32[216,128]{1,0:T(8,128)S(1)} %constant_dynamic-slice_fusion), channel_id=1, source_target_pairs={{0,4},{2,6},{4,0},{6,2},{8,12},{10,14},{12,8},{14,10},{1,5},{3,7},... | collective-permute-start | bytes 331784 | tf_op jit(solution)/shard_map/ppermute | solution.py:576
  13.5 4.3 %copy-start.4 = (bf16[3,432,1024]{2,1,0:T(8,128)(2,1)}, bf16[3,432,1024]{2,1,0:T(8,128)(2,1)S(1)}, u32[]{:S(2)}) copy-start(bf16[3,432,1024]{2,1,0:T(8,128)(2,1)S(1)} %get-tuple-element.54.xs) | copy-start | bytes 7962628
  13.5 6.5 %copy-start.6 = (pred[2,1,256]{2,1,0:T(4,128)(4,1)S(1)}, pred[2,1,256]{2,1,0:T(4,128)(4,1)}, u32[]{:S(2)}) copy-start(pred[2,1,256]{2,1,0:T(4,128)(4,1)} %constant.41) | copy-start | bytes 1540
  13.5 4.8 %collective-permute-start.3 = (f32[216,128]{1,0:T(8,128)S(1)}, f32[216,128]{1,0:T(8,128)S(1)}, u32[]{:S(2)}, u32[]{:S(2)}) collective-permute-start(f32[216,128]{1,0:T(8,128)S(1)} %dynamic-slice_add_fusion), channel_id=1, source_target_pairs={{0,2},{2,0},{4,6},{6,4},{8,10},{10,8},{12,14},{14,12},{1,3},{3,1},... | collective-permute-start | bytes 331784 | tf_op jit(solution)/shard_map/ppermute | solution.py:576
  18.4 11.1 %collective-permute-start.7 = (f32[432,256]{1,0:T(8,128)S(1)}, f32[432,256]{1,0:T(8,128)S(1)}, u32[]{:S(2)}, u32[]{:S(2)}) collective-permute-start(f32[432,256]{1,0:T(8,128)S(1)} %get-tuple-element.61), channel_id=1, source_target_pairs={{0,2},{2,0},{4,6},{6,4},{8,10},{10,8},{12,14},{14,12},{1,3},{3,1},... | collective-permute-start | bytes 1327112 | tf_op jit(solution)/shard_map/ppermute | solution.py:576
  20.0 7.3 %collective-permute-start.4 = (f32[216,128]{1,0:T(8,128)S(1)}, f32[216,128]{1,0:T(8,128)S(1)}, u32[]{:S(2)}, u32[]{:S(2)}) collective-permute-start(f32[216,128]{1,0:T(8,128)S(1)} %add.42), channel_id=1, source_target_pairs={{0,12},{2,14},{4,8},{6,10},{8,4},{10,6},{12,0},{14,2},{1,13},{3,15... | collective-permute-start | bytes 331784 | tf_op jit(solution)/shard_map/ppermute | solution.py:576
  23.6 1.7 %copy-start.5 = (bf16[3,432,1024]{2,1,0:T(8,128)(2,1)S(1)}, bf16[3,432,1024]{2,1,0:T(8,128)(2,1)}, u32[]{:S(2)}) copy-start(bf16[3,432,1024]{2,1,0:T(8,128)(2,1)} %copy-done.4) | copy-start | bytes 7962628
  27.3 18.8 %copy-start.2 = (f32[2,256,128]{2,1,0:T(8,128)S(1)}, f32[2,256,128]{2,1,0:T(8,128)}, u32[]{:S(2)}) copy-start(f32[2,256,128]{2,1,0:T(8,128)} %constant.37.clone.selects_ref) | copy-start | bytes 786436
  27.3 18.8 %copy-start.3 = (f32[8,2,8,512]{3,2,1,0:T(8,128)S(1)}, f32[8,2,8,512]{3,2,1,0:T(8,128)}, u32[]{:S(2)}) copy-start(f32[8,2,8,512]{3,2,1,0:T(8,128)} %constant.36.clone.offsets_ref) | copy-start | bytes 786436
  27.3 4.9 %collective-permute-start.5 = (f32[216,128]{1,0:T(8,128)S(1)}, f32[216,128]{1,0:T(8,128)}, u32[]{:S(2)}, u32[]{:S(2)}) collective-permute-start(f32[216,128]{1,0:T(8,128)S(1)} %add.43), channel_id=1, source_target_pairs={{0,4},{2,6},{4,0},{6,2},{8,12},{10,14},{12,8},{14,10},{1,5},{3,7},... | collective-permute-start | bytes 331784 | tf_op jit(solution)/shard_map/ppermute | solution.py:576
  29.6 16.5 %collective-permute-start.8 = (f32[432,256]{1,0:T(8,128)S(1)}, f32[432,256]{1,0:T(8,128)S(1)}, u32[]{:S(2)}, u32[]{:S(2)}) collective-permute-start(f32[432,256]{1,0:T(8,128)S(1)} %broadcast_select_fusion), channel_id=1, source_target_pairs={{0,0},{2,4},{4,2},{6,8},{8,6},{10,12},{12,10},{14,14},{1,1},{3,5},... | collective-permute-start | bytes 1327112 | tf_op jit(solution)/shard_map/ppermute | solution.py:576
  33.2 2.0 %collective-permute-start.6 = (f32[432,128]{1,0:T(8,128)S(1)}, f32[432,128]{1,0:T(8,128)S(1)}, u32[]{:S(2)}, u32[]{:S(2)}) collective-permute-start(f32[432,128]{1,0:T(8,128)S(1)} %maximum_select_fusion.mine_ref), channel_id=1, source_target_pairs={{0,1},{1,0},{2,3},{3,2},{4,5},{5,4},{6,7},{7,6},{8,9},{9,8},{10,11... | collective-permute-start | bytes 663560 | tf_op jit(solution)/shard_map/ppermute | solution.py:576
  33.3 12.7 %collective-permute-start.9 = (f32[112,128]{1,0:T(8,128)S(1)}, f32[112,128]{1,0:T(8,128)S(1)}, u32[]{:S(2)}, u32[]{:S(2)}) collective-permute-start(f32[112,128]{1,0:T(8,128)S(1)} %get-tuple-element.63), channel_id=1, source_target_pairs={{0,2},{2,6},{4,0},{6,10},{8,4},{10,14},{12,8},{14,12},{1,3},{3,7},... | collective-permute-start | bytes 172040 | tf_op jit(solution)/shard_map/ppermute | solution.py:576
